TPU v7x, 512 devices: a whole 4x8x8 slice. The times are simulated.
512 devices in a mesh: seq: 64 (over x, z, core), tensor: 8 (over y).
Axes of the slice: x: 4, y: 8, z: 8, core: 2. Of those that a mesh axis runs over, the one named last changes fastest.
Arguments:
- signal: bfloat16 [16384, 4096], P('seq', 'tensor'), may hold values from -6 to 6
- kernel_taps: float32 [16384, 4096], P('seq', 'tensor'), may hold values from -3 to 3
- gating: bfloat16 [16384, 4096], P('seq', 'tensor'), may hold values from -6 to 6
- skip_gain: float32 [4096], P('tensor'), may hold values from 0.5 to 1.5
- out_weight: bfloat16 [4096, 4096], P('seq', 'tensor'), may hold values from -0.09375 to 0.09375
Outputs:
- projected: bfloat16 [16384, 4096], P('seq', 'tensor')
All inputs are finite; a program needn't handle non-finite values.
Results may differ from a plain program's by a relative error of at most 0.0049.
Values may be sent and summed in bfloat16 or wider, within the bound.
No kernel may reach another device: no remote copies, remote signals or barrier semaphores. Data moves between devices by JAX's collectives and lax.ppermute only.
A program may use at most 64 MiB of HBM per device.

v0:
```python
import math

import jax
import jax.numpy as jnp
from jax import lax
from jax.sharding import PartitionSpec as P

exact_mode = lax.Precision.HIGHEST


def phase_table(left_index, right_index, modulus):
    pointwise_multiple = left_index[:, None] * right_index[None, :] % modulus
    return pointwise_multiple.astype(jnp.float32) * (2.0 * math.pi / modulus)


def spectral_product(real_part, imag_part, channels):
    sig_real = real_part[..., :channels]
    ker_real = real_part[..., channels:]
    sig_imag = imag_part[..., :channels]
    ker_imag = imag_part[..., channels:]
    prod_real = sig_real * ker_real - sig_imag * ker_imag
    prod_imag = sig_real * ker_imag + sig_imag * ker_real
    return jnp.concatenate([prod_real, prod_imag], axis=-1)


def body(signal, kernel_taps, gating, skip_gain, out_weight):
    seq_count = lax.axis_size("seq")
    seq_rank = lax.axis_index("seq")
    tok_rows = signal.shape[0]
    channels = signal.shape[1]
    sub_rows = tok_rows // seq_count
    double_count = 2 * seq_count
    full_len = 2 * tok_rows * seq_count
    full_weight = lax.all_gather(out_weight, "seq", axis=0, tiled=True)
    values = signal.astype(jnp.float32)
    stacked = jnp.concatenate([values, kernel_taps], axis=1).reshape(1, tok_rows * 2 * channels)
    spread = lax.all_to_all(stacked, "seq", split_axis=1, concat_axis=0, tiled=True)
    block_index = jnp.arange(seq_count, dtype=jnp.int32)
    outer_index = jnp.arange(double_count, dtype=jnp.int32)
    outer_phase = phase_table(outer_index, block_index, double_count)
    first_real = jnp.dot(
        jnp.cos(outer_phase), spread, precision=exact_mode, preferred_element_type=jnp.float32
    )
    first_imag = -jnp.dot(
        jnp.sin(outer_phase), spread, precision=exact_mode, preferred_element_type=jnp.float32
    )
    first_real = first_real.reshape(double_count, sub_rows, 2 * channels)
    first_imag = first_imag.reshape(double_count, sub_rows, 2 * channels)
    global_rows = seq_rank * sub_rows + jnp.arange(sub_rows, dtype=jnp.int32)
    twiddle = phase_table(outer_index, global_rows, full_len)
    tw_cos = jnp.cos(twiddle)[:, :, None]
    tw_sin = jnp.sin(twiddle)[:, :, None]
    tw_real = first_real * tw_cos + first_imag * tw_sin
    tw_imag = first_imag * tw_cos - first_real * tw_sin
    packed = jnp.concatenate([tw_real, tw_imag], axis=2)
    columns = lax.all_to_all(packed, "seq", split_axis=0, concat_axis=1, tiled=True)
    inner_index = jnp.arange(tok_rows, dtype=jnp.int32)
    inner_phase = phase_table(inner_index, inner_index, tok_rows)
    inner_cos = jnp.cos(inner_phase)
    inner_sin = jnp.sin(inner_phase)
    cos_part = jnp.einsum("kb,jbc->jkc", inner_cos, columns, precision=exact_mode)
    sin_part = jnp.einsum("kb,jbc->jkc", inner_sin, columns, precision=exact_mode)
    half = 2 * channels
    spec_real = cos_part[..., :half] + sin_part[..., half:]
    spec_imag = cos_part[..., half:] - sin_part[..., :half]
    fourier_coefficients = jnp.concatenate([spec_real, spec_imag], axis=-1)
    ordered = lax.all_to_all(fourier_coefficients, "seq", split_axis=1, concat_axis=0, tiled=True)
    product_spec = spectral_product(ordered[..., :half], ordered[..., half:], channels)
    product_spec = lax.all_to_all(product_spec, "seq", split_axis=0, concat_axis=1, tiled=True)
    cos_back = jnp.einsum("bk,jkc->jbc", inner_cos, product_spec, precision=exact_mode)
    sin_back = jnp.einsum("bk,jkc->jbc", inner_sin, product_spec, precision=exact_mode)
    back_real = cos_back[..., :channels] - sin_back[..., channels:]
    back_imag = cos_back[..., channels:] + sin_back[..., :channels]
    local_outer = 2 * seq_rank + jnp.arange(2, dtype=jnp.int32)
    back_phase = phase_table(local_outer, inner_index, full_len)
    back_cos = jnp.cos(back_phase)[:, :, None]
    back_sin = jnp.sin(back_phase)[:, :, None]
    turned_real = back_real * back_cos - back_imag * back_sin
    turned_imag = back_imag * back_cos + back_real * back_sin
    turned = jnp.concatenate([turned_real, turned_imag], axis=-1)
    gathered_rows = lax.all_to_all(turned, "seq", split_axis=1, concat_axis=0, tiled=True)
    last_real = gathered_rows[..., :channels].reshape(double_count, sub_rows * channels)
    last_imag = gathered_rows[..., channels:].reshape(double_count, sub_rows * channels)
    last_phase = phase_table(block_index, outer_index, double_count)
    result = jnp.dot(
        jnp.cos(last_phase), last_real, precision=exact_mode, preferred_element_type=jnp.float32
    )
    result = result - jnp.dot(
        jnp.sin(last_phase), last_imag, precision=exact_mode, preferred_element_type=jnp.float32
    )
    result = result * (1.0 / full_len)
    returned = lax.all_to_all(result, "seq", split_axis=0, concat_axis=1, tiled=True)
    convolved = returned.reshape(tok_rows, channels)
    gated_mix = (gating.astype(jnp.float32) * (convolved + skip_gain[None, :] * values)).astype(
        jnp.bfloat16
    )
    projected = jnp.dot(
        lax.all_gather(gated_mix, "tensor", axis=1, tiled=True),
        full_weight,
        preferred_element_type=jnp.float32,
    )
    return projected.astype(jnp.bfloat16)


def solution(mesh):
    placed = (
        P("seq", "tensor"),
        P("seq", "tensor"),
        P("seq", "tensor"),
        P("tensor"),
        P("seq", "tensor"),
    )
    return jax.shard_map(
        body, mesh=mesh, in_specs=placed, out_specs=P("seq", "tensor"), check_vma=False
    )
```

profile of v0, /device:TPU:2, one launch (start us, length us, event | category | flops | bytes accessed | tf_op | source)
XLA Modules:
  0.0 530.5 jit_solution(9656383144322663513)
XLA Ops:
  6.5 1.0 convert_element_type.54
  7.5 1.1 pad_maximum_fusion.4
  8.7 2.2 all_to_all.74
  10.9 13.9 %all-to-all-start = ((f32[1,64,4096]{2,0,1:T(1,128)}), f32[1,64,4096]{2,0,1:T(1,128)S(1)}, u32[]{:S(2)}, u32[]{:S(2)}) async-start(f32[1,64,4096]{2,0,1:T(1,128)} %all_to_all.74), calls=%async_computation | async-start | bytes 2097152 | tf_op jit(solution)/shard_map/all_to_all | solution.py:37
  24.8 0.1 fusion.53
  24.9 27.0 %all-to-all-done = f32[1,64,4096]{2,0,1:T(1,128)S(1)} async-done(((f32[1,64,4096]{2,0,1:T(1,128)}), f32[1,64,4096]{2,0,1:T(1,128)S(1)}, u32[]{:S(2)}, u32[]{:S(2)}) %all-to-all-start) | async-done | bytes 1048608 | tf_op jit(solution)/shard_map/all_to_all | solution.py:37
  51.9 2.4 convolution_negate_fusion
  54.3 1.8 copy.22
  56.2 1.9 copy.23
  58.1 0.6 copy.37
  58.7 2.4 multiply_add_fusion
  61.1 0.5 pad_maximum_fusion
  61.6 2.7 copy.25
  64.3 101.9 %all_to_all.101 = f32[128,4,2048]{2,1,0:T(4,128)S(1)} all-to-all(f32[128,4,2048]{2,1,0:T(4,128)S(1)} %copy.25), channel_id=1, replica_groups=mesh['seq'=64,'tensor'=8] {'seq'}, dimensions={0} | all-to-all | bytes 8388608 | tf_op jit(solution)/shard_map/all_to_all | solution.py:56
  166.2 5.8 %copy.26 = f32[64,2,4,2048]{3,1,2,0:T(2,128)} copy(f32[64,2,4,2048]{3,2,1,0:T(4,128)S(1)} %bitcast.66) | data formatting | bytes 8388608 | tf_op jit(solution)/shard_map/all_to_all | solution.py:56
  172.0 7.3 %copy.27 = f32[2,256,2048]{1,2,0:T(8,128)} copy(f32[2,256,2048]{2,0,1:T(2,128)} %bitcast.67) | data formatting | bytes 8388608 | tf_op jit(solution)/shard_map/all_to_all | solution.py:56
  179.3 0.0 copy-start
  179.3 7.7 %convolution_bitcast_fusion = f32[2,256,2048]{1,2,0:T(8,128)S(1)} fusion(f32[2,256,2048]{1,2,0:T(8,128)} %copy.27), kind=kOutput, calls=%fused_computation.3 | convolution fusion | flops 3222142976 | bytes 8388608 | tf_op jit(solution)/shard_map/kb,jbc->jkc/dot_general | solution.py:62
  186.9 0.0 copy-done
  186.9 4.6 convolution_bitcast_fusion.1
  191.6 0.5 slice_add_fusion
  192.1 2.2 pad_maximum_fusion.1
  194.3 7.4 %copy.29 = f32[2,256,2048]{2,0,1:T(2,128)} copy(f32[2,256,2048]{1,2,0:T(8,128)} %pad_maximum_fusion.1) | data formatting | bytes 8388608 | tf_op jit(solution)/shard_map/concatenate | solution.py:66
  201.7 102.0 %all_to_all.102 = f32[2,256,2048]{2,0,1:T(2,128)S(1)} all-to-all(f32[2,256,2048]{2,0,1:T(2,128)} %copy.29), channel_id=1, replica_groups=mesh['seq'=64,'tensor'=8] {'seq'}, dimensions={1} | all-to-all | bytes 8388608 | tf_op jit(solution)/shard_map/all_to_all | solution.py:67
  303.8 3.9 copy.30
  307.7 0.5 multiply_subtract_fusion.2
  308.2 1.9 pad_maximum_fusion.2
  310.2 7.7 %all-to-all-start.3 = ((f32[128,4,1024]{2,1,0:T(4,128)}), f32[128,4,1024]{2,1,0:T(4,128)S(1)}, u32[]{:S(2)}, u32[]{:S(2)}) async-start(f32[128,4,1024]{2,1,0:T(4,128)} %pad_maximum_fusion.2), calls=%async_computation.3 | async-start | bytes 4194304 | tf_op jit(solution)/shard_map/all_to_all | solution.py:69
  317.9 0.0 all-gather.5.cloned.1.call-start
  318.0 0.7 all-gather.5.cloned.1.call-update
  318.7 0.0 all-gather.3.cloned.1.call-start
  318.7 0.1 fusion.51
  318.9 51.0 %all-to-all-done.3 = f32[128,4,1024]{2,1,0:T(4,128)S(1)} async-done(((f32[128,4,1024]{2,1,0:T(4,128)}), f32[128,4,1024]{2,1,0:T(4,128)S(1)}, u32[]{:S(2)}, u32[]{:S(2)}) %all-to-all-start.3) | async-done | bytes 2097184 | tf_op jit(solution)/shard_map/all_to_all | solution.py:69
  369.8 3.3 copy.31
  373.1 2.7 copy.32
  375.9 2.9 convolution_bitcast_fusion.2
  378.7 2.9 convolution_bitcast_fusion.3
  381.6 0.3 multiply_subtract_fusion.1
  381.9 0.1 pad_maximum_fusion.3
  382.0 2.4 copy.34
  384.5 62.7 %all_to_all.103 = f32[2,256,1024]{2,0,1:T(2,128)S(1)} all-to-all(f32[2,256,1024]{2,0,1:T(2,128)} %copy.34), channel_id=1, replica_groups=mesh['seq'=64,'tensor'=8] {'seq'}, dimensions={1} | all-to-all | bytes 4194304 | tf_op jit(solution)/shard_map/all_to_all | solution.py:81
  447.1 1.0 copy.35
  448.1 0.4 fusion.87
  448.5 0.3 copy.39
  448.8 0.3 copy.40
  449.2 0.8 fusion.34
  450.0 0.8 fusion.1
  450.8 0.0 copy-start.1
  450.8 0.0 copy-start.2
  450.8 0.0 copy-start.3
  450.8 0.5 copy.36
  451.4 23.2 %all_to_all.104 = f32[64,1,2048]{2,1,0:T(1,128)S(1)} all-to-all(f32[64,1,2048]{2,1,0:T(1,128)S(1)} %copy.36), channel_id=1, replica_groups=mesh['seq'=64,'tensor'=8] {'seq'}, dimensions={0} | all-to-all | bytes 1048576 | tf_op jit(solution)/shard_map/all_to_all | solution.py:92
  474.5 1.2 reduce
  475.8 0.1 reshape.145
  475.9 0.0 copy-done.1
  476.0 0.0 copy-done.2
  476.0 0.0 copy-done.3
  476.0 0.8 multiply_convert_fusion
  476.8 0.0 all-gather.3.cloned.1.call-update
  476.8 0.0 all-gather.5.cloned.1.call-done
  476.8 41.6 %all-gather.3.cloned.1.call-done = bf16[256,4096]{1,0:T(8,128)(2,1)} async-done(((bf16[256,512]{1,0:T(8,128)(2,1)}), bf16[256,4096]{1,0:T(8,128)(2,1)}) %all-gather.3.cloned.1.call-update) | async-done | bytes 2097168 | tf_op jit(solution)/shard_map/all_gather | solution.py:98
  518.4 4.8 convolution_convert_fusion
  (2 shorter events, 0.0 us)
Async XLA Ops:
  10.9 41.0 %all-to-all-start = ((f32[1,64,4096]{2,0,1:T(1,128)}), f32[1,64,4096]{2,0,1:T(1,128)S(1)}, u32[]{:S(2)}, u32[]{:S(2)}) async-start(f32[1,64,4096]{2,0,1:T(1,128)} %all_to_all.74), calls=%async_computation | async-start | bytes 2097152 | tf_op jit(solution)/shard_map/all_to_all | solution.py:37
  179.3 7.7 %copy-start = (f32[2,256,2048]{1,2,0:T(8,128)S(1)}, f32[2,256,2048]{1,2,0:T(8,128)}, u32[]{:S(2)}) copy-start(f32[2,256,2048]{1,2,0:T(8,128)} %copy.27) | copy-start | bytes 12582916
  310.2 59.6 %all-to-all-start.3 = ((f32[128,4,1024]{2,1,0:T(4,128)}), f32[128,4,1024]{2,1,0:T(4,128)S(1)}, u32[]{:S(2)}, u32[]{:S(2)}) async-start(f32[128,4,1024]{2,1,0:T(4,128)} %pad_maximum_fusion.2), calls=%async_computation.3 | async-start | bytes 4194304 | tf_op jit(solution)/shard_map/all_to_all | solution.py:69
  317.9 158.9 %all-gather.5.cloned.1.call-start = ((), (), s32[]{:S(2)}) async-start(), calls=%async_computation.7 | async-start | bytes 4259840 | tf_op jit(solution)/shard_map/all_gather | solution.py:34
  318.7 199.8 %all-gather.3.cloned.1.call-start = ((), (), s32[]{:S(2)}) async-start(), calls=%async_computation.6 | async-start | bytes 2359296 | tf_op jit(solution)/shard_map/all_gather | solution.py:98
  450.8 25.2 %copy-start.1 = (bf16[256,512]{1,0:T(8,128)(2,1)S(1)}, bf16[256,512]{1,0:T(8,128)(2,1)}, u32[]{:S(2)}) copy-start(bf16[256,512]{1,0:T(8,128)(2,1)} %param.5) | copy-start | bytes 786436
  450.8 25.2 %copy-start.2 = (bf16[256,512]{1,0:T(8,128)(2,1)S(1)}, bf16[256,512]{1,0:T(8,128)(2,1)}, u32[]{:S(2)}) copy-start(bf16[256,512]{1,0:T(8,128)(2,1)} %param.7) | copy-start | bytes 786436
  450.8 25.2 %copy-start.3 = (f32[512]{0:T(512)S(1)}, f32[512]{0:T(512)}, u32[]{:S(2)}) copy-start(f32[512]{0:T(512)} %param.8) | copy-start | bytes 6148
Sparse Core Ops, SparseCore 0:
  322.1 94.8 all-gather.4
  476.9 41.4 all-gather.2
where the time goes:
time: 540 us; the launch traced here: 530 us
  blocking collectives  290 us (54%)
  waiting for transfers between devices  120 us (22%)
  local copies, waits for them, and re-layouts  44.9 us (8%)
  matrix products  29.1 us (5%)
  starting transfers between devices  21.7 us (4%)
  between operations  14.2 us (3%)
  other arithmetic  10.6 us (2%)
    all_to_all x1, blocking collectives, body(): lax.all_to_all(fourier_coefficients, 'seq', split_axis=1, concat_axis=0,...  102 us
    all_to_all x1, blocking collectives, body(): lax.all_to_all(packed, 'seq', split_axis=0, concat_axis=1, tiled=True)  102 us
    all_to_all x1, blocking collectives, body(): lax.all_to_all(turned, 'seq', split_axis=1, concat_axis=0, tiled=True)  62.7 us
    all_to_all x1, waiting for transfers between devices, body(): lax.all_to_all(product_spec, 'seq', split_axis=0, concat_axis=1, tiled=True)  51 us
    all_gather x1, waiting for transfers between devices, body(): lax.all_gather(gated_mix, 'tensor', axis=1, tiled=True)  41.6 us
    all_to_all x1, waiting for transfers between devices, body(): lax.all_to_all(stacked, 'seq', split_axis=1, concat_axis=0, tiled=True)  27 us
    all_to_all x1, blocking collectives, body(): lax.all_to_all(result, 'seq', split_axis=0, concat_axis=1, tiled=True)  23.2 us
    all_to_all x1, starting transfers between devices, body(): lax.all_to_all(stacked, 'seq', split_axis=1, concat_axis=0, tiled=True)  13.9 us
  transfers between devices with their start and end apart: 4, of which 3 were waited for; matrix products, arithmetic and copies ran while one was open for 4% of the time, Pallas kernels for 0%

commit v1 on v0

v1 whole, which is shorter than its diff:
```python
import math

import jax
import jax.numpy as jnp
import ml_dtypes
import numpy as np
from jax import lax
from jax.experimental import pallas as pl
from jax.experimental.pallas import tpu as pltpu
from jax.sharding import PartitionSpec as P

F32 = jnp.float32
BF16 = jnp.bfloat16
MIB = 1024 * 1024


def split_np(table):
    high = table.astype(ml_dtypes.bfloat16)
    low = (table - high.astype(np.float64)).astype(ml_dtypes.bfloat16)
    return high, low


def phases(left, right, modulus):
    return (left[:, None] * right[None, :] % modulus) * (2.0 * math.pi / modulus)


def dft_tables(blocks, inner):
    outer = 2 * blocks
    length = outer * inner
    freqs = blocks + 1
    held = -(-freqs // 8) * 8
    f = np.arange(freqs)
    b = np.arange(blocks)
    i = np.arange(inner)
    first = np.zeros((2 * held, blocks))
    angle = phases(f, b, outer)
    first[:freqs] = np.cos(angle)
    first[held : held + freqs] = -np.sin(angle)
    first = np.concatenate(split_np(first), axis=1)
    turn = np.zeros((2, held, inner), np.float32)
    turn[0, :freqs] = np.cos(phases(f, i, length))
    turn[1, :freqs] = np.sin(phases(f, i, length))
    angle = phases(i, i, inner)
    cos, sin = np.cos(angle), np.sin(angle)
    mid_high, mid_low = split_np(np.block([[cos, -sin], [sin, cos]]))
    mid = np.concatenate([mid_high, mid_high, mid_low], axis=0)
    weight = np.where((f == 0) | (f == blocks), 1.0, 2.0) / length
    last = np.zeros((blocks, 2 * held))
    angle = phases(b, f, outer)
    last[:, :freqs] = np.cos(angle) * weight
    last[:, held : held + freqs] = -np.sin(angle) * weight
    last_high, last_low = split_np(last)
    last = np.concatenate([last_high, last_high, last_low], axis=1)
    return first, turn, mid, last


def split(values):
    high = values.astype(BF16)
    low = (values - high.astype(F32)).astype(BF16)
    return high, low


def pack_kernel(signal_ref, taps_ref, *refs):
    tables, (out_ref, *kept), (signal, taps, arrived) = refs[:4], refs[4:9], refs[9:]
    moves = [(signal_ref, signal), (taps_ref, taps), *zip(tables, kept)]
    copies = [pltpu.make_async_copy(src, dst, arrived.at[n]) for n, (src, dst) in enumerate(moves)]
    for copy in copies:
        copy.start()
    tokens, channels = signal.shape
    copies[0].wait()
    sig = signal[...].astype(F32).T.reshape(channels // 8, 8, tokens)
    copies[1].wait()
    ker = taps[...].T.reshape(channels // 8, 8, tokens)
    out_ref[...] = jnp.concatenate([sig, ker], axis=1).astype(BF16)
    for copy in copies[2:]:
        copy.wait()


def conv_kernel(x_ref, first_ref, turn_ref, mid_ref, last_ref, out_ref, flat, cat, spec, back):
    blocks, rows, inner = x_ref.shape
    chans = rows // 2
    held = turn_ref.shape[1]
    lanes = flat.shape[1]
    halves = inner // lanes
    span = blocks * rows
    for h in range(halves):
        flat[h * span : (h + 1) * span, :] = (
            x_ref[:, :, h * lanes : (h + 1) * lanes].astype(F32).reshape(span, lanes)
        )
    for c in range(chans):
        parts = []
        for row in (c, chans + c):
            x = jnp.concatenate(
                [flat[pl.ds(h * span + row, blocks, stride=rows), :] for h in range(halves)], axis=1
            ).astype(BF16)
            a = jnp.dot(first_ref[...], jnp.concatenate([x, x], axis=0), preferred_element_type=F32)
            real, imag = a[:held], a[held:]
            parts.append(
                jnp.concatenate(
                    [real * turn_ref[0] + imag * turn_ref[1], imag * turn_ref[0] - real * turn_ref[1]], axis=1
                )
            )
        high, low = split(jnp.concatenate(parts, axis=0))
        here = pl.ds(c * 2 * held, 2 * held)
        cat[here, : 2 * inner] = high
        cat[here, 2 * inner : 4 * inner] = low
        cat[here, 4 * inner :] = high
    spec[...] = jnp.dot(cat[...], mid_ref[...], preferred_element_type=F32)
    for c in range(0, chans, 2):
        parts = []
        for one in (c, c + 1):
            s = spec[pl.ds(one * 2 * held, held), :]
            k = spec[pl.ds(one * 2 * held + held, held), :]
            sr, si, kr, ki = s[:, :inner], s[:, inner:], k[:, :inner], k[:, inner:]
            parts.append(jnp.concatenate([sr * kr - si * ki, -(sr * ki + si * kr)], axis=1))
        high, low = split(jnp.concatenate(parts, axis=0))
        here = pl.ds(c * held, 2 * held)
        cat[here, : 2 * inner] = high
        cat[here, 2 * inner : 4 * inner] = low
        cat[here, 4 * inner :] = high
    half = chans * held
    spec[:half, :] = jnp.dot(cat[:half, :], mid_ref[...], preferred_element_type=F32)
    for c in range(chans):
        q = spec[pl.ds(c * held, held), :]
        qr, qi = q[:, :inner], -q[:, inner:]
        v = jnp.concatenate(
            [qr * turn_ref[0] - qi * turn_ref[1], qr * turn_ref[1] + qi * turn_ref[0]], axis=0
        )
        high, low = split(v)
        y = jnp.dot(last_ref[...], jnp.concatenate([high, low, high], axis=0), preferred_element_type=F32)
        for h in range(inner // lanes):
            back[pl.ds(h * chans + c, blocks, stride=rows), :] = y[:, h * lanes : (h + 1) * lanes]
    out_ref[...] = back[...].reshape(blocks, rows, lanes).astype(BF16)


def gate_kernel(back_ref, signal_ref, gating_ref, skip_ref, out_ref):
    groups, rows, lanes = back_ref.shape
    chans = 8
    tokens, channels = signal_ref.shape
    y = back_ref[...].astype(F32)
    for h in range(tokens // lanes):
        conv = y[:, h * chans : (h + 1) * chans, :].reshape(channels, lanes).T
        here = pl.ds(h * lanes, lanes)
        mixed = conv + skip_ref[...] * signal_ref[here, :].astype(F32)
        out_ref[here, :] = (gating_ref[here, :].astype(F32) * mixed).astype(BF16)


def project_kernel(index_ref, *refs):
    *pieces, w_ref, total_ref, last_ref, held, arrived = refs
    depth = held.shape[1]
    copies = []
    for n in range(len(pieces) + 1):
        rows = pl.ds(pl.multiple_of(index_ref[n] * depth, depth), depth)
        target = held.at[n] if n < len(pieces) else last_ref
        copies.append(pltpu.make_async_copy(w_ref.at[rows, :], target, arrived.at[n]))
        copies[n].start()
    total = None
    for n, piece in enumerate(pieces):
        copies[n].wait()
        product = jnp.dot(piece[...], held[n], preferred_element_type=F32)
        total = product if total is None else total + product
    total_ref[...] = total
    copies[-1].wait()


def finish_kernel(total_ref, up_ref, down_ref, w_ref, out_ref):
    piece = jnp.concatenate([up_ref[...], down_ref[...]], axis=0)
    product = jnp.dot(piece, w_ref[...], preferred_element_type=F32)
    out_ref[...] = (total_ref[...] + product).astype(BF16)


def vmem_limit(mebibytes):
    return pltpu.CompilerParams(vmem_limit_bytes=mebibytes * MIB)


def body(signal, kernel_taps, gating, skip_gain, out_weight):
    seq_count = lax.axis_size("seq")
    ring = lax.axis_size("tensor")
    tokens, channels = signal.shape
    full_weight = lax.all_gather(out_weight, "seq", axis=0, tiled=True)
    tables = [jnp.asarray(table) for table in dft_tables(seq_count, tokens)]
    vmem = pl.BlockSpec(memory_space=pltpu.VMEM)
    anywhere = pl.BlockSpec(memory_space=pl.ANY)
    packed, *tables = pl.pallas_call(
        pack_kernel,
        in_specs=[anywhere] * 6,
        out_specs=[vmem] * 5,
        out_shape=[jax.ShapeDtypeStruct((channels // 8, 16, tokens), BF16)]
        + [jax.ShapeDtypeStruct(table.shape, table.dtype) for table in tables],
        scratch_shapes=[
            pltpu.VMEM((tokens, channels), BF16),
            pltpu.VMEM((tokens, channels), F32),
            pltpu.SemaphoreType.DMA((6,)),
        ],
        compiler_params=vmem_limit(48),
    )(signal, kernel_taps, *tables)
    spread = lax.all_to_all(packed, "seq", split_axis=0, concat_axis=0, tiled=True)
    held = tables[1].shape[1]
    convolved = pl.pallas_call(
        conv_kernel,
        out_shape=jax.ShapeDtypeStruct((seq_count, 16, 128), BF16),
        scratch_shapes=[
            pltpu.VMEM((tokens // 128 * seq_count * 16, 128), F32),
            pltpu.VMEM((16 * held, 6 * tokens), BF16),
            pltpu.VMEM((16 * held, 2 * tokens), F32),
            pltpu.VMEM((seq_count * 16, 128), F32),
        ],
        compiler_params=vmem_limit(24),
    )(spread, *tables)
    returned = lax.all_to_all(convolved, "seq", split_axis=0, concat_axis=0, tiled=True)
    gated = pl.pallas_call(
        gate_kernel, out_shape=jax.ShapeDtypeStruct((tokens, channels), BF16), compiler_params=vmem_limit(8)
    )(returned, signal, gating, skip_gain.reshape(1, channels))
    up_pairs = [(t, (t + 1) % ring) for t in range(ring)]
    down_pairs = [(t, (t - 1) % ring) for t in range(ring)]
    pieces, offsets = [gated], [0]
    up = down = gated
    for n in range(1, ring // 2):
        up = lax.ppermute(up, "tensor", up_pairs)
        down = lax.ppermute(down, "tensor", down_pairs)
        pieces += [up, down]
        offsets += [-n, n]
    up = lax.ppermute(up[: tokens // 2], "tensor", up_pairs)
    down = lax.ppermute(down[tokens // 2 :], "tensor", down_pairs)
    offsets.append(ring // 2)
    index = (lax.axis_index("tensor") + jnp.asarray(offsets, jnp.int32)) % ring
    total, last_weight = pl.pallas_call(
        project_kernel,
        in_specs=[pl.BlockSpec(memory_space=pltpu.SMEM)] + [vmem] * len(pieces) + [anywhere],
        out_specs=[vmem] * 2,
        out_shape=[
            jax.ShapeDtypeStruct((tokens, channels), F32),
            jax.ShapeDtypeStruct((channels, channels), BF16),
        ],
        scratch_shapes=[
            pltpu.VMEM((len(pieces), channels, channels), BF16),
            pltpu.SemaphoreType.DMA((ring,)),
        ],
        compiler_params=vmem_limit(48),
    )(index, *pieces, full_weight)
    return pl.pallas_call(
        finish_kernel, out_shape=jax.ShapeDtypeStruct((tokens, channels), BF16), compiler_params=vmem_limit(8)
    )(total, up, down, last_weight)


def solution(mesh):
    placed = (
        P("seq", "tensor"),
        P("seq", "tensor"),
        P("seq", "tensor"),
        P("tensor"),
        P("seq", "tensor"),
    )
    return jax.shard_map(
        body, mesh=mesh, in_specs=placed, out_specs=P("seq", "tensor"), check_vma=False
    )
```

time: 540 us -> 121 us (0.22)
  the two profiles are of different devices: /device:TPU:2 before, /device:TPU:24 now
where the time goes in v1:
time: 121 us
  blocking collectives  50 us (41%)
  starting transfers between devices  29.2 us (24%)
  between operations  13.6 us (11%)
  waiting for transfers between devices  12.6 us (10%)
  Pallas kernels  9.27 us (8%)
  local copies, waits for them, and re-layouts  5.94 us (5%)
    all_to_all x1, blocking collectives, body(): lax.all_to_all(packed, 'seq', split_axis=0, concat_axis=0, tiled=True)  31.7 us
    all_to_all x1, blocking collectives, body(): lax.all_to_all(convolved, 'seq', split_axis=0, concat_axis=0, tiled=True)  18.4 us
    ppermute x3, starting transfers between devices, body(): up = lax.ppermute(up, 'tensor', up_pairs)  15.9 us
    ppermute x3, waiting for transfers between devices, body(): up = lax.ppermute(up, 'tensor', up_pairs)  8.96 us
    unnamed x18, local copies, waits for them, and re-layouts  5.92 us
    ppermute x3, starting transfers between devices, body(): down = lax.ppermute(down, 'tensor', down_pairs)  5.76 us
    ppermute x1, starting transfers between devices, body(): up = lax.ppermute(up[:tokens // 2], 'tensor', up_pairs)  5.6 us
    pallas_call x1, Pallas kernels, body(): pl.pallas_call(conv_kernel, out_shape=jax.ShapeDtypeStruct((seq_count, 16...  4.08 us
  transfers between devices with their start and end apart: 9, of which 4 were waited for; matrix products, arithmetic and copies ran while one was open for 0% of the time, Pallas kernels for 7%

profile of v1, /device:TPU:24, one launch (start us, length us, event | category | flops | bytes accessed | tf_op | source)
XLA Modules:
  0.0 120.6 jit_solution(9468904877962027142)
XLA Ops:
  6.5 0.0 all-gather.2.cloned.1.call-start
  6.5 0.7 all-gather.2.cloned.1.call-update
  7.3 0.0 copy-start
  7.3 1.4 %copy-done = bf16[1536,512]{1,0:T(8,128)(2,1)S(1)} copy-done((bf16[1536,512]{1,0:T(8,128)(2,1)S(1)}, bf16[1536,512]{1,0:T(8,128)(2,1)}, u32[]{:S(2)}) %copy-start) | copy-done | bytes 1572888
  8.7 0.0 copy-start.1
  8.7 0.9 copy-done.1
  9.6 0.0 copy-start.2
  9.6 1.0 copy-done.2
  10.7 0.0 copy-start.4
  10.7 0.9 copy-done.4
  11.6 0.0 copy-start.5
  11.6 0.8 copy-done.5
  12.4 0.0 copy-start.6
  12.4 0.8 copy-done.6
  13.2 0.8 shard_map.100
  14.0 31.7 %all_to_all.10.x_ref = bf16[64,16,256]{2,1,0:T(8,128)(2,1)S(1)} all-to-all(bf16[64,16,256]{2,1,0:T(8,128)(2,1)S(1)} %get-tuple-element.12), channel_id=1, replica_groups=mesh['seq'=64,'tensor'=8] {'seq'}, dimensions={0} | all-to-all | bytes 1048576 | tf_op jit(solution)/shard_map/all_to_all | solution.py:197
  45.7 0.0 copy-start.3
  45.7 0.0 copy-start.7
  45.7 4.1 %shard_map.101 = bf16[64,16,128]{2,1,0:T(8,128)(2,1)S(1)} custom-call(bf16[64,16,256]{2,1,0:T(8,128)(2,1)S(1)} %all_to_all.10.x_ref, bf16[144,128]{1,0:T(8,128)(2,1)S(1)} %get-tuple-element.13.first_ref, f32[2,72,256]{2,1,0:T(8,128)S(1)} %get-tuple-element.14.turn_ref, bf16[1536,512]{1,0:T(8,128)(2,1)S(1)} %get-tuple-element.15.mid_ref, ...), custom_call_target="tpu_custom_call" | custom-call | tf_op jit(solution)/shard_map/pallas_call | solution.py:199
  49.8 0.0 copy-start.8
  49.8 18.4 %all_to_all.11.back_ref = bf16[64,16,128]{2,1,0:T(8,128)(2,1)S(1)} all-to-all(bf16[64,16,128]{2,1,0:T(8,128)(2,1)S(1)} %shard_map.101), channel_id=1, replica_groups=mesh['seq'=64,'tensor'=8] {'seq'}, dimensions={0} | all-to-all | bytes 524288 | tf_op jit(solution)/shard_map/all_to_all | solution.py:210
  68.2 0.0 copy-done.3
  68.2 0.0 copy-done.7
  68.2 0.2 shard_map.102.refs_0_
  68.3 4.7 %collective-permute-start = (bf16[256,512]{1,0:T(8,128)(2,1)S(1)}, bf16[256,512]{1,0:T(8,128)(2,1)S(1)}, u32[]{:S(2)}, u32[]{:S(2)}) collective-permute-start(bf16[256,512]{1,0:T(8,128)(2,1)S(1)} %shard_map.102.refs_0_), channel_id=1, source_target_pairs={{0,1},{1,2},{2,3},{3,4},{4,5},{5,6},{6,7},{7,0},{8,9},{9,10},{10,1... | collective-permute-start | bytes 786440 | tf_op jit(solution)/shard_map/ppermute | solution.py:219
  73.0 1.9 %collective-permute-start.1 = (bf16[256,512]{1,0:T(8,128)(2,1)S(1)}, bf16[256,512]{1,0:T(8,128)(2,1)S(1)}, u32[]{:S(2)}, u32[]{:S(2)}) collective-permute-start(bf16[256,512]{1,0:T(8,128)(2,1)S(1)} %shard_map.102.refs_0_), channel_id=1, source_target_pairs={{0,7},{1,0},{2,1},{3,2},{4,3},{5,4},{6,5},{7,6},{8,15},{9,8},{10,9... | collective-permute-start | bytes 786440 | tf_op jit(solution)/shard_map/ppermute | solution.py:220
  75.0 3.8 %collective-permute-done.refs_1_ = bf16[256,512]{1,0:T(8,128)(2,1)S(1)} collective-permute-done((bf16[256,512]{1,0:T(8,128)(2,1)S(1)}, bf16[256,512]{1,0:T(8,128)(2,1)S(1)}, u32[]{:S(2)}, u32[]{:S(2)}) %collective-permute-start) | collective-permute-done | bytes 262176 | tf_op jit(solution)/shard_map/ppermute | solution.py:219
  78.8 5.6 %collective-permute-start.2 = (bf16[256,512]{1,0:T(8,128)(2,1)S(1)}, bf16[256,512]{1,0:T(8,128)(2,1)S(1)}, u32[]{:S(2)}, u32[]{:S(2)}) collective-permute-start(bf16[256,512]{1,0:T(8,128)(2,1)S(1)} %collective-permute-done.refs_1_), channel_id=1, source_target_pairs={{0,1},{1,2},{2,3},{3,4},{4,5},{5,6},{6,7},{7,0},{8,9},{9,10},{10,1... | collective-permute-start | bytes 786440 | tf_op jit(solution)/shard_map/ppermute | solution.py:219
  84.4 0.0 collective-permute-done.1.refs_2_
  84.4 1.9 %collective-permute-start.3 = (bf16[256,512]{1,0:T(8,128)(2,1)S(1)}, bf16[256,512]{1,0:T(8,128)(2,1)S(1)}, u32[]{:S(2)}, u32[]{:S(2)}) collective-permute-start(bf16[256,512]{1,0:T(8,128)(2,1)S(1)} %collective-permute-done.1.refs_2_), channel_id=1, source_target_pairs={{0,7},{1,0},{2,1},{3,2},{4,3},{5,4},{6,5},{7,6},{8,15},{9,8},{10,9... | collective-permute-start | bytes 786440 | tf_op jit(solution)/shard_map/ppermute | solution.py:220
  86.3 3.0 %collective-permute-done.2.refs_3_ = bf16[256,512]{1,0:T(8,128)(2,1)S(1)} collective-permute-done((bf16[256,512]{1,0:T(8,128)(2,1)S(1)}, bf16[256,512]{1,0:T(8,128)(2,1)S(1)}, u32[]{:S(2)}, u32[]{:S(2)}) %collective-permute-start.2) | collective-permute-done | bytes 262176 | tf_op jit(solution)/shard_map/ppermute | solution.py:219
  89.3 5.6 %collective-permute-start.4 = (bf16[256,512]{1,0:T(8,128)(2,1)S(1)}, bf16[256,512]{1,0:T(8,128)(2,1)S(1)}, u32[]{:S(2)}, u32[]{:S(2)}) collective-permute-start(bf16[256,512]{1,0:T(8,128)(2,1)S(1)} %collective-permute-done.2.refs_3_), channel_id=1, source_target_pairs={{0,1},{1,2},{2,3},{3,4},{4,5},{5,6},{6,7},{7,0},{8,9},{9,10},{10,1... | collective-permute-start | bytes 786440 | tf_op jit(solution)/shard_map/ppermute | solution.py:219
  94.9 0.0 collective-permute-done.3.refs_4_
  94.9 1.9 %collective-permute-start.5 = (bf16[256,512]{1,0:T(8,128)(2,1)S(1)}, bf16[256,512]{1,0:T(8,128)(2,1)S(1)}, u32[]{:S(2)}, u32[]{:S(2)}) collective-permute-start(bf16[256,512]{1,0:T(8,128)(2,1)S(1)} %collective-permute-done.3.refs_4_), channel_id=1, source_target_pairs={{0,7},{1,0},{2,1},{3,2},{4,3},{5,4},{6,5},{7,6},{8,15},{9,8},{10,9... | collective-permute-start | bytes 786440 | tf_op jit(solution)/shard_map/ppermute | solution.py:220
  96.9 2.1 %collective-permute-done.4.refs_5_ = bf16[256,512]{1,0:T(8,128)(2,1)S(1)} collective-permute-done((bf16[256,512]{1,0:T(8,128)(2,1)S(1)}, bf16[256,512]{1,0:T(8,128)(2,1)S(1)}, u32[]{:S(2)}, u32[]{:S(2)}) %collective-permute-start.4) | collective-permute-done | bytes 262176 | tf_op jit(solution)/shard_map/ppermute | solution.py:219
  99.0 5.6 %collective-permute-start.6 = (bf16[128,512]{1,0:T(8,128)(2,1)S(1)}, bf16[128,512]{1,0:T(8,128)(2,1)S(1)}, u32[]{:S(2)}, u32[]{:S(2)}) collective-permute-start(bf16[128,512]{1,0:T(8,128)(2,1)S(1)} %slice.8), channel_id=1, source_target_pairs={{0,1},{1,2},{2,3},{3,4},{4,5},{5,6},{6,7},{7,0},{8,9},{9,10},{10,1... | collective-permute-start | bytes 393224 | tf_op jit(solution)/shard_map/ppermute | solution.py:223
  104.6 0.0 collective-permute-done.5.refs_6_
  104.6 1.9 %collective-permute-start.7 = (bf16[128,512]{1,0:T(8,128)(2,1)S(1)}, bf16[128,512]{1,0:T(8,128)(2,1)S(1)}, u32[]{:S(2)}, u32[]{:S(2)}) collective-permute-start(bf16[128,512]{1,0:T(8,128)(2,1)S(1)} %slice.9), channel_id=1, source_target_pairs={{0,7},{1,0},{2,1},{3,2},{4,3},{5,4},{6,5},{7,6},{8,15},{9,8},{10,9... | collective-permute-start | bytes 393224 | tf_op jit(solution)/shard_map/ppermute | solution.py:224
  106.6 0.0 copy-done.8
  106.6 0.0 all-gather.2.cloned.1.call-done.refs_7_
  106.6 3.2 %shard_map.103 = (f32[256,512]{1,0:T(8,128)S(1)}, bf16[512,512]{1,0:T(8,128)(2,1)S(1)}) custom-call(s32[8]{0:T(128)S(1)} %and_select_fusion.index_ref, bf16[256,512]{1,0:T(8,128)(2,1)S(1)} %shard_map.102.refs_0_, bf16[256,512]{1,0:T(8,128)(2,1)S(1)} %collective-permute-done.refs_1_, bf16[256,512]{1,0:T(8,128)(2,1)S(1)} %collective-permute-done.1.refs_2_, ...), custom_call_target="tpu_custom_call" | custom-call | tf_op jit(solution)/shard_map/pallas_call | solution.py:227
  109.8 0.0 collective-permute-done.6.up_ref
  109.8 2.9 %collective-permute-done.7.down_ref = bf16[128,512]{1,0:T(8,128)(2,1)S(1)} collective-permute-done((bf16[128,512]{1,0:T(8,128)(2,1)S(1)}, bf16[128,512]{1,0:T(8,128)(2,1)S(1)}, u32[]{:S(2)}, u32[]{:S(2)}) %collective-permute-start.7) | collective-permute-done | bytes 131104 | tf_op jit(solution)/shard_map/ppermute | solution.py:224
  112.7 1.0 shard_map.104
  (3 shorter events, 0.0 us)
Async XLA Ops:
  6.5 100.1 %all-gather.2.cloned.1.call-start = ((), (), s32[]{:S(2)}) async-start(), calls=%async_computation.2 | async-start | bytes 4259840 | tf_op jit(solution)/shard_map/all_gather | solution.py:180
  7.3 1.4 %copy-start = (bf16[1536,512]{1,0:T(8,128)(2,1)S(1)}, bf16[1536,512]{1,0:T(8,128)(2,1)}, u32[]{:S(2)}) copy-start(bf16[1536,512]{1,0:T(8,128)(2,1)} %constant.31.clone.refs_2_) | copy-start | bytes 4718596
  8.7 0.9 copy-start.1
  9.6 1.0 copy-start.2
  10.7 0.9 copy-start.4
  11.6 0.8 copy-start.5
  12.4 0.8 copy-start.6
  45.7 22.5 %copy-start.3 = (bf16[256,512]{1,0:T(8,128)(2,1)S(1)}, bf16[256,512]{1,0:T(8,128)(2,1)}, u32[]{:S(2)}) copy-start(bf16[256,512]{1,0:T(8,128)(2,1)} %gating_ref.1) | copy-start | bytes 786436
  45.7 22.5 %copy-start.7 = (f32[512]{0:T(512)S(1)}, f32[512]{0:T(512)}, u32[]{:S(2)}) copy-start(f32[512]{0:T(512)} %param.13) | copy-start | bytes 6148
  49.8 56.8 %copy-start.8 = (s32[8]{0:T(128)S(1)}, s32[8]{0:T(128)}, u32[]{:S(2)}) copy-start(s32[8]{0:T(128)} %constant.33.clone) | copy-start | bytes 100
  68.3 10.5 %collective-permute-start = (bf16[256,512]{1,0:T(8,128)(2,1)S(1)}, bf16[256,512]{1,0:T(8,128)(2,1)S(1)}, u32[]{:S(2)}, u32[]{:S(2)}) collective-permute-start(bf16[256,512]{1,0:T(8,128)(2,1)S(1)} %shard_map.102.refs_0_), channel_id=1, source_target_pairs={{0,1},{1,2},{2,3},{3,4},{4,5},{5,6},{6,7},{7,0},{8,9},{9,10},{10,1... | collective-permute-start | bytes 786440 | tf_op jit(solution)/shard_map/ppermute | solution.py:219
  73.0 11.4 %collective-permute-start.1 = (bf16[256,512]{1,0:T(8,128)(2,1)S(1)}, bf16[256,512]{1,0:T(8,128)(2,1)S(1)}, u32[]{:S(2)}, u32[]{:S(2)}) collective-permute-start(bf16[256,512]{1,0:T(8,128)(2,1)S(1)} %shard_map.102.refs_0_), channel_id=1, source_target_pairs={{0,7},{1,0},{2,1},{3,2},{4,3},{5,4},{6,5},{7,6},{8,15},{9,8},{10,9... | collective-permute-start | bytes 786440 | tf_op jit(solution)/shard_map/ppermute | solution.py:220
  78.8 10.5 %collective-permute-start.2 = (bf16[256,512]{1,0:T(8,128)(2,1)S(1)}, bf16[256,512]{1,0:T(8,128)(2,1)S(1)}, u32[]{:S(2)}, u32[]{:S(2)}) collective-permute-start(bf16[256,512]{1,0:T(8,128)(2,1)S(1)} %collective-permute-done.refs_1_), channel_id=1, source_target_pairs={{0,1},{1,2},{2,3},{3,4},{4,5},{5,6},{6,7},{7,0},{8,9},{9,10},{10,1... | collective-permute-start | bytes 786440 | tf_op jit(solution)/shard_map/ppermute | solution.py:219
  84.4 10.5 %collective-permute-start.3 = (bf16[256,512]{1,0:T(8,128)(2,1)S(1)}, bf16[256,512]{1,0:T(8,128)(2,1)S(1)}, u32[]{:S(2)}, u32[]{:S(2)}) collective-permute-start(bf16[256,512]{1,0:T(8,128)(2,1)S(1)} %collective-permute-done.1.refs_2_), channel_id=1, source_target_pairs={{0,7},{1,0},{2,1},{3,2},{4,3},{5,4},{6,5},{7,6},{8,15},{9,8},{10,9... | collective-permute-start | bytes 786440 | tf_op jit(solution)/shard_map/ppermute | solution.py:220
  89.3 9.7 %collective-permute-start.4 = (bf16[256,512]{1,0:T(8,128)(2,1)S(1)}, bf16[256,512]{1,0:T(8,128)(2,1)S(1)}, u32[]{:S(2)}, u32[]{:S(2)}) collective-permute-start(bf16[256,512]{1,0:T(8,128)(2,1)S(1)} %collective-permute-done.2.refs_3_), channel_id=1, source_target_pairs={{0,1},{1,2},{2,3},{3,4},{4,5},{5,6},{6,7},{7,0},{8,9},{9,10},{10,1... | collective-permute-start | bytes 786440 | tf_op jit(solution)/shard_map/ppermute | solution.py:219
  94.9 9.7 %collective-permute-start.5 = (bf16[256,512]{1,0:T(8,128)(2,1)S(1)}, bf16[256,512]{1,0:T(8,128)(2,1)S(1)}, u32[]{:S(2)}, u32[]{:S(2)}) collective-permute-start(bf16[256,512]{1,0:T(8,128)(2,1)S(1)} %collective-permute-done.3.refs_4_), channel_id=1, source_target_pairs={{0,7},{1,0},{2,1},{3,2},{4,3},{5,4},{6,5},{7,6},{8,15},{9,8},{10,9... | collective-permute-start | bytes 786440 | tf_op jit(solution)/shard_map/ppermute | solution.py:220
  99.0 10.8 %collective-permute-start.6 = (bf16[128,512]{1,0:T(8,128)(2,1)S(1)}, bf16[128,512]{1,0:T(8,128)(2,1)S(1)}, u32[]{:S(2)}, u32[]{:S(2)}) collective-permute-start(bf16[128,512]{1,0:T(8,128)(2,1)S(1)} %slice.8), channel_id=1, source_target_pairs={{0,1},{1,2},{2,3},{3,4},{4,5},{5,6},{6,7},{7,0},{8,9},{9,10},{10,1... | collective-permute-start | bytes 393224 | tf_op jit(solution)/shard_map/ppermute | solution.py:223
  104.6 8.1 %collective-permute-start.7 = (bf16[128,512]{1,0:T(8,128)(2,1)S(1)}, bf16[128,512]{1,0:T(8,128)(2,1)S(1)}, u32[]{:S(2)}, u32[]{:S(2)}) collective-permute-start(bf16[128,512]{1,0:T(8,128)(2,1)S(1)} %slice.9), channel_id=1, source_target_pairs={{0,7},{1,0},{2,1},{3,2},{4,3},{5,4},{6,5},{7,6},{8,15},{9,8},{10,9... | collective-permute-start | bytes 393224 | tf_op jit(solution)/shard_map/ppermute | solution.py:224
Sparse Core Ops, SparseCore 0:
  10.7 89.8 all-gather.1

commit v2 on v1

--- a/solution.py
+++ b/solution.py
@@ -1,3 +1,4 @@
+import functools
 import math
 
 import jax
@@ -36,22 +37,27 @@
     angle = phases(f, b, outer)
     first[:freqs] = np.cos(angle)
     first[held : held + freqs] = -np.sin(angle)
-    first = np.concatenate(split_np(first), axis=1)
-    turn = np.zeros((2, held, inner), np.float32)
-    turn[0, :freqs] = np.cos(phases(f, i, length))
-    turn[1, :freqs] = np.sin(phases(f, i, length))
+    turn = np.zeros((2 * held, inner))
+    turn[:freqs] = np.cos(phases(f, i, length))
+    turn[held : held + freqs] = np.sin(phases(f, i, length))
     angle = phases(i, i, inner)
-    cos, sin = np.cos(angle), np.sin(angle)
-    mid_high, mid_low = split_np(np.block([[cos, -sin], [sin, cos]]))
-    mid = np.concatenate([mid_high, mid_high, mid_low], axis=0)
+    mid = np.concatenate([np.cos(angle), np.sin(angle)], axis=1)
     weight = np.where((f == 0) | (f == blocks), 1.0, 2.0) / length
     last = np.zeros((blocks, 2 * held))
     angle = phases(b, f, outer)
     last[:, :freqs] = np.cos(angle) * weight
     last[:, held : held + freqs] = -np.sin(angle) * weight
     last_high, last_low = split_np(last)
-    last = np.concatenate([last_high, last_high, last_low], axis=1)
-    return first, turn, mid, last
+    parts = [
+        np.concatenate(split_np(mid), axis=0),
+        np.concatenate(split_np(turn), axis=1),
+        np.concatenate(split_np(first), axis=1),
+        np.concatenate([last_high, last_high, last_low], axis=1),
+    ]
+    width = 2 * inner
+    table = np.concatenate([np.pad(part, ((0, 0), (0, width - part.shape[1]))) for part in parts], axis=0)
+    ends = np.cumsum([part.shape[0] for part in parts])
+    return table, [(int(end) - part.shape[0], int(end), part.shape[1]) for end, part in zip(ends, parts)]
 
 
 def split(values):
@@ -60,26 +66,32 @@
     return high, low
 
 
-def pack_kernel(signal_ref, taps_ref, *refs):
-    tables, (out_ref, *kept), (signal, taps, arrived) = refs[:4], refs[4:9], refs[9:]
-    moves = [(signal_ref, signal), (taps_ref, taps), *zip(tables, kept)]
-    copies = [pltpu.make_async_copy(src, dst, arrived.at[n]) for n, (src, dst) in enumerate(moves)]
-    for copy in copies:
-        copy.start()
-    tokens, channels = signal.shape
-    copies[0].wait()
-    sig = signal[...].astype(F32).T.reshape(channels // 8, 8, tokens)
-    copies[1].wait()
-    ker = taps[...].T.reshape(channels // 8, 8, tokens)
+def pack_kernel(signal_ref, taps_ref, out_ref):
+    tokens, channels = signal_ref.shape
+    sig = signal_ref[...].astype(F32).T.reshape(channels // 8, 8, tokens)
+    ker = taps_ref[...].T.reshape(channels // 8, 8, tokens)
     out_ref[...] = jnp.concatenate([sig, ker], axis=1).astype(BF16)
-    for copy in copies[2:]:
-        copy.wait()
-
-
-def conv_kernel(x_ref, first_ref, turn_ref, mid_ref, last_ref, out_ref, flat, cat, spec, back):
+
+
+def spread_mid(short, mid):
+    inner = short.shape[1] // 2
+    for n, rows in enumerate((0, 0, inner)):
+        cos, sin = short[rows : rows + inner, :inner], short[rows : rows + inner, inner:]
+        mid[2 * n * inner : (2 * n + 1) * inner, :inner] = cos
+        mid[2 * n * inner : (2 * n + 1) * inner, inner:] = -sin
+        mid[(2 * n + 1) * inner : (2 * n + 2) * inner, :inner] = sin
+        mid[(2 * n + 1) * inner : (2 * n + 2) * inner, inner:] = cos
+
+
+def conv_kernel(places, x_ref, table_ref, out_ref, flat, cat, spec, back, mid, turn):
+    parts = [table_ref.at[pl.ds(start, end - start), pl.ds(0, width)] for start, end, width in places]
+    short_ref, turn_ref, first_ref, last_ref = parts
+    held = turn.shape[0] // 2
+    spread_mid(short_ref, mid)
+    turn[...] = turn_ref[:, : turn.shape[1]].astype(F32) + turn_ref[:, turn.shape[1] :].astype(F32)
+    cos_ref, sin_ref = turn.at[pl.ds(0, held)], turn.at[pl.ds(held, held)]
     blocks, rows, inner = x_ref.shape
     chans = rows // 2
-    held = turn_ref.shape[1]
     lanes = flat.shape[1]
     halves = inner // lanes
     span = blocks * rows
@@ -97,7 +109,7 @@
             real, imag = a[:held], a[held:]
             parts.append(
                 jnp.concatenate(
-                    [real * turn_ref[0] + imag * turn_ref[1], imag * turn_ref[0] - real * turn_ref[1]], axis=1
+                    [real * cos_ref[...] + imag * sin_ref[...], imag * cos_ref[...] - real * sin_ref[...]], axis=1
                 )
             )
         high, low = split(jnp.concatenate(parts, axis=0))
@@ -105,7 +117,7 @@
         cat[here, : 2 * inner] = high
         cat[here, 2 * inner : 4 * inner] = low
         cat[here, 4 * inner :] = high
-    spec[...] = jnp.dot(cat[...], mid_ref[...], preferred_element_type=F32)
+    spec[...] = jnp.dot(cat[...], mid[...], preferred_element_type=F32)
     for c in range(0, chans, 2):
         parts = []
         for one in (c, c + 1):
@@ -119,12 +131,12 @@
         cat[here, 2 * inner : 4 * inner] = low
         cat[here, 4 * inner :] = high
     half = chans * held
-    spec[:half, :] = jnp.dot(cat[:half, :], mid_ref[...], preferred_element_type=F32)
+    spec[:half, :] = jnp.dot(cat[:half, :], mid[...], preferred_element_type=F32)
     for c in range(chans):
         q = spec[pl.ds(c * held, held), :]
         qr, qi = q[:, :inner], -q[:, inner:]
         v = jnp.concatenate(
-            [qr * turn_ref[0] - qi * turn_ref[1], qr * turn_ref[1] + qi * turn_ref[0]], axis=0
+            [qr * cos_ref[...] - qi * sin_ref[...], qr * sin_ref[...] + qi * cos_ref[...]], axis=0
         )
         high, low = split(v)
         y = jnp.dot(last_ref[...], jnp.concatenate([high, low, high], axis=0), preferred_element_type=F32)
@@ -178,35 +190,30 @@
     ring = lax.axis_size("tensor")
     tokens, channels = signal.shape
     full_weight = lax.all_gather(out_weight, "seq", axis=0, tiled=True)
-    tables = [jnp.asarray(table) for table in dft_tables(seq_count, tokens)]
+    table, places = dft_tables(seq_count, tokens)
+    turn_rows = places[1][1] - places[1][0]
+    held = turn_rows // 2
     vmem = pl.BlockSpec(memory_space=pltpu.VMEM)
-    anywhere = pl.BlockSpec(memory_space=pl.ANY)
-    packed, *tables = pl.pallas_call(
+    packed = pl.pallas_call(
         pack_kernel,
-        in_specs=[anywhere] * 6,
-        out_specs=[vmem] * 5,
-        out_shape=[jax.ShapeDtypeStruct((channels // 8, 16, tokens), BF16)]
-        + [jax.ShapeDtypeStruct(table.shape, table.dtype) for table in tables],
-        scratch_shapes=[
-            pltpu.VMEM((tokens, channels), BF16),
-            pltpu.VMEM((tokens, channels), F32),
-            pltpu.SemaphoreType.DMA((6,)),
-        ],
-        compiler_params=vmem_limit(48),
-    )(signal, kernel_taps, *tables)
+        out_shape=jax.ShapeDtypeStruct((channels // 8, 16, tokens), BF16),
+        compiler_params=vmem_limit(8),
+    )(signal, kernel_taps)
+    packed, table = lax.optimization_barrier((packed, jnp.asarray(table)))
     spread = lax.all_to_all(packed, "seq", split_axis=0, concat_axis=0, tiled=True)
-    held = tables[1].shape[1]
     convolved = pl.pallas_call(
-        conv_kernel,
+        functools.partial(conv_kernel, places),
         out_shape=jax.ShapeDtypeStruct((seq_count, 16, 128), BF16),
         scratch_shapes=[
             pltpu.VMEM((tokens // 128 * seq_count * 16, 128), F32),
             pltpu.VMEM((16 * held, 6 * tokens), BF16),
             pltpu.VMEM((16 * held, 2 * tokens), F32),
             pltpu.VMEM((seq_count * 16, 128), F32),
+            pltpu.VMEM((6 * tokens, 2 * tokens), BF16),
+            pltpu.VMEM((turn_rows, tokens), F32),
         ],
         compiler_params=vmem_limit(24),
-    )(spread, *tables)
+    )(spread, table)
     returned = lax.all_to_all(convolved, "seq", split_axis=0, concat_axis=0, tiled=True)
     gated = pl.pallas_call(
         gate_kernel, out_shape=jax.ShapeDtypeStruct((tokens, channels), BF16), compiler_params=vmem_limit(8)
@@ -226,7 +233,7 @@
     index = (lax.axis_index("tensor") + jnp.asarray(offsets, jnp.int32)) % ring
     total, last_weight = pl.pallas_call(
         project_kernel,
-        in_specs=[pl.BlockSpec(memory_space=pltpu.SMEM)] + [vmem] * len(pieces) + [anywhere],
+        in_specs=[pl.BlockSpec(memory_space=pltpu.SMEM)] + [vmem] * len(pieces) + [pl.BlockSpec(memory_space=pl.ANY)],
         out_specs=[vmem] * 2,
         out_shape=[
             jax.ShapeDtypeStruct((tokens, channels), F32),

time: 121 us -> 117 us (0.967)
  local copies, waits for them, and re-layouts: 5.94 us -> 3.19 us
    unnamed x18 -> x14, local copies, waits for them, and re-layouts: 5.92 us -> 3.17 us
  transfers between devices with their start and end apart: 9 -> 9, of which waited for: 4 -> 4; matrix products, arithmetic and copies ran while one was open for 0% -> 0% of each run, Pallas kernels for 7% -> 6%
where the time goes in v2:
time: 117 us
  blocking collectives  49.4 us (42%)
  starting transfers between devices  29.2 us (25%)
  between operations  13.6 us (12%)
  waiting for transfers between devices  12.9 us (11%)
  Pallas kernels  8.52 us (7%)
  local copies, waits for them, and re-layouts  3.19 us (3%)
    all_to_all x1, blocking collectives, body(): lax.all_to_all(packed, 'seq', split_axis=0, concat_axis=0, tiled=True)  31.3 us
    all_to_all x1, blocking collectives, body(): lax.all_to_all(convolved, 'seq', split_axis=0, concat_axis=0, tiled=True)  18.1 us
    ppermute x3, starting transfers between devices, body(): up = lax.ppermute(up, 'tensor', up_pairs)  15.9 us
    ppermute x3, waiting for transfers between devices, body(): up = lax.ppermute(up, 'tensor', up_pairs)  9.26 us
    ppermute x3, starting transfers between devices, body(): down = lax.ppermute(down, 'tensor', down_pairs)  5.76 us
    ppermute x1, starting transfers between devices, body(): up = lax.ppermute(up[:tokens // 2], 'tensor', up_pairs)  5.6 us
    pallas_call x1, Pallas kernels, body(): pl.pallas_call(functools.partial(conv_kernel, places), out_shape=jax.Shap...  3.97 us
    pallas_call x1, Pallas kernels, body(): pl.pallas_call(project_kernel, in_specs=[pl.BlockSpec(memory_space=pltpu....  3.19 us
  transfers between devices with their start and end apart: 9, of which 4 were waited for; matrix products, arithmetic and copies ran while one was open for 0% of the time, Pallas kernels for 6%

profile of v2, /device:TPU:24, one launch (start us, length us, event | category | flops | bytes accessed | tf_op | source)
XLA Modules:
  0.0 116.8 jit_solution(2230595668950015946)
XLA Ops:
  6.5 0.0 copy-start.6
  6.5 0.0 copy-start.5
  6.5 0.0 all-gather.2.cloned.1.call-start
  6.5 0.7 all-gather.2.cloned.1.call-update
  7.3 0.0 copy-start
  7.3 0.9 copy-done
  8.2 0.0 copy-start.3
  8.2 1.0 copy-done.3
  9.3 0.0 copy-start.1
  9.3 0.0 copy-start.4
  9.3 0.2 shard_map.73
  9.5 31.3 %all_to_all.10.x_ref = bf16[64,16,256]{2,1,0:T(8,128)(2,1)S(1)} all-to-all(bf16[64,16,256]{2,1,0:T(8,128)(2,1)S(1)} %shard_map.73), channel_id=1, replica_groups=mesh['seq'=64,'tensor'=8] {'seq'}, dimensions={0} | all-to-all | bytes 1048576 | tf_op jit(solution)/shard_map/all_to_all | solution.py:203
  40.8 0.0 copy-start.2
  40.8 1.2 %copy-done.2 = bf16[864,512]{1,0:T(8,128)(2,1)S(1)} copy-done((bf16[864,512]{1,0:T(8,128)(2,1)S(1)}, bf16[864,512]{1,0:T(8,128)(2,1)}, u32[]{:S(2)}) %copy-start.2) | copy-done | bytes 884760
  42.0 4.0 %shard_map.74 = bf16[64,16,128]{2,1,0:T(8,128)(2,1)S(1)} custom-call(bf16[64,16,256]{2,1,0:T(8,128)(2,1)S(1)} %all_to_all.10.x_ref, bf16[864,512]{1,0:T(8,128)(2,1)S(1)} %copy-done.2), custom_call_target="tpu_custom_call" | custom-call | tf_op jit(solution)/shard_map/pallas_call | solution.py:204
  46.0 18.1 %all_to_all.11.back_ref = bf16[64,16,128]{2,1,0:T(8,128)(2,1)S(1)} all-to-all(bf16[64,16,128]{2,1,0:T(8,128)(2,1)S(1)} %shard_map.74), channel_id=1, replica_groups=mesh['seq'=64,'tensor'=8] {'seq'}, dimensions={0} | all-to-all | bytes 524288 | tf_op jit(solution)/shard_map/all_to_all | solution.py:217
  64.0 0.0 copy-done.5
  64.0 0.0 copy-done.1
  64.0 0.0 copy-done.4
  64.0 0.2 shard_map.75.refs_0_
  64.2 4.7 %collective-permute-start = (bf16[256,512]{1,0:T(8,128)(2,1)S(1)}, bf16[256,512]{1,0:T(8,128)(2,1)S(1)}, u32[]{:S(2)}, u32[]{:S(2)}) collective-permute-start(bf16[256,512]{1,0:T(8,128)(2,1)S(1)} %shard_map.75.refs_0_), channel_id=1, source_target_pairs={{0,1},{1,2},{2,3},{3,4},{4,5},{5,6},{6,7},{7,0},{8,9},{9,10},{10,1... | collective-permute-start | bytes 786440 | tf_op jit(solution)/shard_map/ppermute | solution.py:226
  68.9 1.9 %collective-permute-start.1 = (bf16[256,512]{1,0:T(8,128)(2,1)S(1)}, bf16[256,512]{1,0:T(8,128)(2,1)S(1)}, u32[]{:S(2)}, u32[]{:S(2)}) collective-permute-start(bf16[256,512]{1,0:T(8,128)(2,1)S(1)} %shard_map.75.refs_0_), channel_id=1, source_target_pairs={{0,7},{1,0},{2,1},{3,2},{4,3},{5,4},{6,5},{7,6},{8,15},{9,8},{10,9... | collective-permute-start | bytes 786440 | tf_op jit(solution)/shard_map/ppermute | solution.py:227
  70.8 3.9 %collective-permute-done.refs_1_ = bf16[256,512]{1,0:T(8,128)(2,1)S(1)} collective-permute-done((bf16[256,512]{1,0:T(8,128)(2,1)S(1)}, bf16[256,512]{1,0:T(8,128)(2,1)S(1)}, u32[]{:S(2)}, u32[]{:S(2)}) %collective-permute-start) | collective-permute-done | bytes 262176 | tf_op jit(solution)/shard_map/ppermute | solution.py:226
  74.7 5.6 %collective-permute-start.2 = (bf16[256,512]{1,0:T(8,128)(2,1)S(1)}, bf16[256,512]{1,0:T(8,128)(2,1)S(1)}, u32[]{:S(2)}, u32[]{:S(2)}) collective-permute-start(bf16[256,512]{1,0:T(8,128)(2,1)S(1)} %collective-permute-done.refs_1_), channel_id=1, source_target_pairs={{0,1},{1,2},{2,3},{3,4},{4,5},{5,6},{6,7},{7,0},{8,9},{9,10},{10,1... | collective-permute-start | bytes 786440 | tf_op jit(solution)/shard_map/ppermute | solution.py:226
  80.3 0.0 collective-permute-done.1.refs_2_
  80.3 1.9 %collective-permute-start.3 = (bf16[256,512]{1,0:T(8,128)(2,1)S(1)}, bf16[256,512]{1,0:T(8,128)(2,1)S(1)}, u32[]{:S(2)}, u32[]{:S(2)}) collective-permute-start(bf16[256,512]{1,0:T(8,128)(2,1)S(1)} %collective-permute-done.1.refs_2_), channel_id=1, source_target_pairs={{0,7},{1,0},{2,1},{3,2},{4,3},{5,4},{6,5},{7,6},{8,15},{9,8},{10,9... | collective-permute-start | bytes 786440 | tf_op jit(solution)/shard_map/ppermute | solution.py:227
  82.3 3.1 %collective-permute-done.2.refs_3_ = bf16[256,512]{1,0:T(8,128)(2,1)S(1)} collective-permute-done((bf16[256,512]{1,0:T(8,128)(2,1)S(1)}, bf16[256,512]{1,0:T(8,128)(2,1)S(1)}, u32[]{:S(2)}, u32[]{:S(2)}) %collective-permute-start.2) | collective-permute-done | bytes 262176 | tf_op jit(solution)/shard_map/ppermute | solution.py:226
  85.4 5.6 %collective-permute-start.4 = (bf16[256,512]{1,0:T(8,128)(2,1)S(1)}, bf16[256,512]{1,0:T(8,128)(2,1)S(1)}, u32[]{:S(2)}, u32[]{:S(2)}) collective-permute-start(bf16[256,512]{1,0:T(8,128)(2,1)S(1)} %collective-permute-done.2.refs_3_), channel_id=1, source_target_pairs={{0,1},{1,2},{2,3},{3,4},{4,5},{5,6},{6,7},{7,0},{8,9},{9,10},{10,1... | collective-permute-start | bytes 786440 | tf_op jit(solution)/shard_map/ppermute | solution.py:226
  91.0 0.0 collective-permute-done.3.refs_4_
  91.0 1.9 %collective-permute-start.5 = (bf16[256,512]{1,0:T(8,128)(2,1)S(1)}, bf16[256,512]{1,0:T(8,128)(2,1)S(1)}, u32[]{:S(2)}, u32[]{:S(2)}) collective-permute-start(bf16[256,512]{1,0:T(8,128)(2,1)S(1)} %collective-permute-done.3.refs_4_), channel_id=1, source_target_pairs={{0,7},{1,0},{2,1},{3,2},{4,3},{5,4},{6,5},{7,6},{8,15},{9,8},{10,9... | collective-permute-start | bytes 786440 | tf_op jit(solution)/shard_map/ppermute | solution.py:227
  93.0 2.2 %collective-permute-done.4.refs_5_ = bf16[256,512]{1,0:T(8,128)(2,1)S(1)} collective-permute-done((bf16[256,512]{1,0:T(8,128)(2,1)S(1)}, bf16[256,512]{1,0:T(8,128)(2,1)S(1)}, u32[]{:S(2)}, u32[]{:S(2)}) %collective-permute-start.4) | collective-permute-done | bytes 262176 | tf_op jit(solution)/shard_map/ppermute | solution.py:226
  95.2 5.6 %collective-permute-start.6 = (bf16[128,512]{1,0:T(8,128)(2,1)S(1)}, bf16[128,512]{1,0:T(8,128)(2,1)S(1)}, u32[]{:S(2)}, u32[]{:S(2)}) collective-permute-start(bf16[128,512]{1,0:T(8,128)(2,1)S(1)} %slice.8), channel_id=1, source_target_pairs={{0,1},{1,2},{2,3},{3,4},{4,5},{5,6},{6,7},{7,0},{8,9},{9,10},{10,1... | collective-permute-start | bytes 393224 | tf_op jit(solution)/shard_map/ppermute | solution.py:230
  100.8 0.0 collective-permute-done.5.refs_6_
  100.8 1.9 %collective-permute-start.7 = (bf16[128,512]{1,0:T(8,128)(2,1)S(1)}, bf16[128,512]{1,0:T(8,128)(2,1)S(1)}, u32[]{:S(2)}, u32[]{:S(2)}) collective-permute-start(bf16[128,512]{1,0:T(8,128)(2,1)S(1)} %slice.9), channel_id=1, source_target_pairs={{0,7},{1,0},{2,1},{3,2},{4,3},{5,4},{6,5},{7,6},{8,15},{9,8},{10,9... | collective-permute-start | bytes 393224 | tf_op jit(solution)/shard_map/ppermute | solution.py:231
  102.8 0.0 copy-done.6
  102.8 0.0 all-gather.2.cloned.1.call-done.refs_7_
  102.8 3.2 %shard_map.76 = (f32[256,512]{1,0:T(8,128)S(1)}, bf16[512,512]{1,0:T(8,128)(2,1)S(1)}) custom-call(s32[8]{0:T(128)S(1)} %and_select_fusion.index_ref, bf16[256,512]{1,0:T(8,128)(2,1)S(1)} %shard_map.75.refs_0_, bf16[256,512]{1,0:T(8,128)(2,1)S(1)} %collective-permute-done.refs_1_, bf16[256,512]{1,0:T(8,128)(2,1)S(1)} %collective-permute-done.1.refs_2_, ...), custom_call_target="tpu_custom_call" | custom-call | tf_op jit(solution)/shard_map/pallas_call | solution.py:234
  106.0 0.0 collective-permute-done.6.up_ref
  106.0 2.9 %collective-permute-done.7.down_ref = bf16[128,512]{1,0:T(8,128)(2,1)S(1)} collective-permute-done((bf16[128,512]{1,0:T(8,128)(2,1)S(1)}, bf16[128,512]{1,0:T(8,128)(2,1)S(1)}, u32[]{:S(2)}, u32[]{:S(2)}) %collective-permute-start.7) | collective-permute-done | bytes 131104 | tf_op jit(solution)/shard_map/ppermute | solution.py:231
  108.9 1.0 shard_map.77
  (3 shorter events, 0.0 us)
Async XLA Ops:
  6.5 96.2 %copy-start.6 = (s32[8]{0:T(128)S(1)}, s32[8]{0:T(128)}, u32[]{:S(2)}) copy-start(s32[8]{0:T(128)} %constant.24.clone) | copy-start | bytes 100
  6.5 57.5 %copy-start.5 = (f32[512]{0:T(512)S(1)}, f32[512]{0:T(512)}, u32[]{:S(2)}) copy-start(f32[512]{0:T(512)} %param.10) | copy-start | bytes 6148
  6.5 96.3 %all-gather.2.cloned.1.call-start = ((), (), s32[]{:S(2)}) async-start(), calls=%async_computation.2 | async-start | bytes 4259840 | tf_op jit(solution)/shard_map/all_gather | solution.py:192
  7.3 1.0 copy-start
  8.2 1.0 copy-start.3
  9.3 54.8 %copy-start.1 = (bf16[256,512]{1,0:T(8,128)(2,1)S(1)}, bf16[256,512]{1,0:T(8,128)(2,1)}, u32[]{:S(2)}) copy-start(bf16[256,512]{1,0:T(8,128)(2,1)} %signal_ref.3) | copy-start | bytes 786436
  9.3 54.8 %copy-start.4 = (bf16[256,512]{1,0:T(8,128)(2,1)S(1)}, bf16[256,512]{1,0:T(8,128)(2,1)}, u32[]{:S(2)}) copy-start(bf16[256,512]{1,0:T(8,128)(2,1)} %gating_ref.1) | copy-start | bytes 786436
  40.8 1.2 %copy-start.2 = (bf16[864,512]{1,0:T(8,128)(2,1)S(1)}, bf16[864,512]{1,0:T(8,128)(2,1)}, u32[]{:S(2)}) copy-start(bf16[864,512]{1,0:T(8,128)(2,1)} %constant.23.clone.table_ref) | copy-start | bytes 2654212
  64.2 10.6 %collective-permute-start = (bf16[256,512]{1,0:T(8,128)(2,1)S(1)}, bf16[256,512]{1,0:T(8,128)(2,1)S(1)}, u32[]{:S(2)}, u32[]{:S(2)}) collective-permute-start(bf16[256,512]{1,0:T(8,128)(2,1)S(1)} %shard_map.75.refs_0_), channel_id=1, source_target_pairs={{0,1},{1,2},{2,3},{3,4},{4,5},{5,6},{6,7},{7,0},{8,9},{9,10},{10,1... | collective-permute-start | bytes 786440 | tf_op jit(solution)/shard_map/ppermute | solution.py:226
  68.9 11.4 %collective-permute-start.1 = (bf16[256,512]{1,0:T(8,128)(2,1)S(1)}, bf16[256,512]{1,0:T(8,128)(2,1)S(1)}, u32[]{:S(2)}, u32[]{:S(2)}) collective-permute-start(bf16[256,512]{1,0:T(8,128)(2,1)S(1)} %shard_map.75.refs_0_), channel_id=1, source_target_pairs={{0,7},{1,0},{2,1},{3,2},{4,3},{5,4},{6,5},{7,6},{8,15},{9,8},{10,9... | collective-permute-start | bytes 786440 | tf_op jit(solution)/shard_map/ppermute | solution.py:227
  74.7 10.7 %collective-permute-start.2 = (bf16[256,512]{1,0:T(8,128)(2,1)S(1)}, bf16[256,512]{1,0:T(8,128)(2,1)S(1)}, u32[]{:S(2)}, u32[]{:S(2)}) collective-permute-start(bf16[256,512]{1,0:T(8,128)(2,1)S(1)} %collective-permute-done.refs_1_), channel_id=1, source_target_pairs={{0,1},{1,2},{2,3},{3,4},{4,5},{5,6},{6,7},{7,0},{8,9},{9,10},{10,1... | collective-permute-start | bytes 786440 | tf_op jit(solution)/shard_map/ppermute | solution.py:226
  80.3 10.7 %collective-permute-start.3 = (bf16[256,512]{1,0:T(8,128)(2,1)S(1)}, bf16[256,512]{1,0:T(8,128)(2,1)S(1)}, u32[]{:S(2)}, u32[]{:S(2)}) collective-permute-start(bf16[256,512]{1,0:T(8,128)(2,1)S(1)} %collective-permute-done.1.refs_2_), channel_id=1, source_target_pairs={{0,7},{1,0},{2,1},{3,2},{4,3},{5,4},{6,5},{7,6},{8,15},{9,8},{10,9... | collective-permute-start | bytes 786440 | tf_op jit(solution)/shard_map/ppermute | solution.py:227
  85.4 9.8 %collective-permute-start.4 = (bf16[256,512]{1,0:T(8,128)(2,1)S(1)}, bf16[256,512]{1,0:T(8,128)(2,1)S(1)}, u32[]{:S(2)}, u32[]{:S(2)}) collective-permute-start(bf16[256,512]{1,0:T(8,128)(2,1)S(1)} %collective-permute-done.2.refs_3_), channel_id=1, source_target_pairs={{0,1},{1,2},{2,3},{3,4},{4,5},{5,6},{6,7},{7,0},{8,9},{9,10},{10,1... | collective-permute-start | bytes 786440 | tf_op jit(solution)/shard_map/ppermute | solution.py:226
  91.0 9.8 %collective-permute-start.5 = (bf16[256,512]{1,0:T(8,128)(2,1)S(1)}, bf16[256,512]{1,0:T(8,128)(2,1)S(1)}, u32[]{:S(2)}, u32[]{:S(2)}) collective-permute-start(bf16[256,512]{1,0:T(8,128)(2,1)S(1)} %collective-permute-done.3.refs_4_), channel_id=1, source_target_pairs={{0,7},{1,0},{2,1},{3,2},{4,3},{5,4},{6,5},{7,6},{8,15},{9,8},{10,9... | collective-permute-start | bytes 786440 | tf_op jit(solution)/shard_map/ppermute | solution.py:227
  95.2 10.8 %collective-permute-start.6 = (bf16[128,512]{1,0:T(8,128)(2,1)S(1)}, bf16[128,512]{1,0:T(8,128)(2,1)S(1)}, u32[]{:S(2)}, u32[]{:S(2)}) collective-permute-start(bf16[128,512]{1,0:T(8,128)(2,1)S(1)} %slice.8), channel_id=1, source_target_pairs={{0,1},{1,2},{2,3},{3,4},{4,5},{5,6},{6,7},{7,0},{8,9},{9,10},{10,1... | collective-permute-start | bytes 393224 | tf_op jit(solution)/shard_map/ppermute | solution.py:230
  100.8 8.1 %collective-permute-start.7 = (bf16[128,512]{1,0:T(8,128)(2,1)S(1)}, bf16[128,512]{1,0:T(8,128)(2,1)S(1)}, u32[]{:S(2)}, u32[]{:S(2)}) collective-permute-start(bf16[128,512]{1,0:T(8,128)(2,1)S(1)} %slice.9), channel_id=1, source_target_pairs={{0,7},{1,0},{2,1},{3,2},{4,3},{5,4},{6,5},{7,6},{8,15},{9,8},{10,9... | collective-permute-start | bytes 393224 | tf_op jit(solution)/shard_map/ppermute | solution.py:231
Sparse Core Ops, SparseCore 0:
  10.7 90.0 all-gather.1

commit v3 on v2

--- a/solution.py
+++ b/solution.py
@@ -75,7 +75,7 @@
 
 def spread_mid(short, mid):
     inner = short.shape[1] // 2
-    for n, rows in enumerate((0, 0, inner)):
+    for n, rows in enumerate((0, inner)):
         cos, sin = short[rows : rows + inner, :inner], short[rows : rows + inner, inner:]
         mid[2 * n * inner : (2 * n + 1) * inner, :inner] = cos
         mid[2 * n * inner : (2 * n + 1) * inner, inner:] = -sin
@@ -112,11 +112,10 @@
                     [real * cos_ref[...] + imag * sin_ref[...], imag * cos_ref[...] - real * sin_ref[...]], axis=1
                 )
             )
-        high, low = split(jnp.concatenate(parts, axis=0))
+        both = jnp.concatenate(parts, axis=0).astype(BF16)
         here = pl.ds(c * 2 * held, 2 * held)
-        cat[here, : 2 * inner] = high
-        cat[here, 2 * inner : 4 * inner] = low
-        cat[here, 4 * inner :] = high
+        cat[here, : 2 * inner] = both
+        cat[here, 2 * inner :] = both
     spec[...] = jnp.dot(cat[...], mid[...], preferred_element_type=F32)
     for c in range(0, chans, 2):
         parts = []
@@ -125,11 +124,10 @@
             k = spec[pl.ds(one * 2 * held + held, held), :]
             sr, si, kr, ki = s[:, :inner], s[:, inner:], k[:, :inner], k[:, inner:]
             parts.append(jnp.concatenate([sr * kr - si * ki, -(sr * ki + si * kr)], axis=1))
-        high, low = split(jnp.concatenate(parts, axis=0))
+        both = jnp.concatenate(parts, axis=0).astype(BF16)
         here = pl.ds(c * held, 2 * held)
-        cat[here, : 2 * inner] = high
-        cat[here, 2 * inner : 4 * inner] = low
-        cat[here, 4 * inner :] = high
+        cat[here, : 2 * inner] = both
+        cat[here, 2 * inner :] = both
     half = chans * held
     spec[:half, :] = jnp.dot(cat[:half, :], mid[...], preferred_element_type=F32)
     for c in range(chans):
@@ -206,10 +204,10 @@
         out_shape=jax.ShapeDtypeStruct((seq_count, 16, 128), BF16),
         scratch_shapes=[
             pltpu.VMEM((tokens // 128 * seq_count * 16, 128), F32),
-            pltpu.VMEM((16 * held, 6 * tokens), BF16),
+            pltpu.VMEM((16 * held, 4 * tokens), BF16),
             pltpu.VMEM((16 * held, 2 * tokens), F32),
             pltpu.VMEM((seq_count * 16, 128), F32),
-            pltpu.VMEM((6 * tokens, 2 * tokens), BF16),
+            pltpu.VMEM((4 * tokens, 2 * tokens), BF16),
             pltpu.VMEM((turn_rows, tokens), F32),
         ],
         compiler_params=vmem_limit(24),

time: 117 us -> 117 us (level)
  the two profiles are of different devices: /device:TPU:24 before, /device:TPU:30 now
where the time goes in v3:
time: 117 us; the launch traced here: 116 us
  blocking collectives  49.6 us (42%)
  starting transfers between devices  29.2 us (25%)
  between operations  13.6 us (12%)
  waiting for transfers between devices  13 us (11%)
  Pallas kernels  7.51 us (6%)
  local copies, waits for them, and re-layouts  3.19 us (3%)
    all_to_all x1, blocking collectives, body(): lax.all_to_all(packed, 'seq', split_axis=0, concat_axis=0, tiled=True)  31.1 us
    all_to_all x1, blocking collectives, body(): lax.all_to_all(convolved, 'seq', split_axis=0, concat_axis=0, tiled=True)  18.5 us
    ppermute x3, starting transfers between devices, body(): up = lax.ppermute(up, 'tensor', up_pairs)  15.9 us
    ppermute x3, waiting for transfers between devices, body(): up = lax.ppermute(up, 'tensor', up_pairs)  9.38 us
    ppermute x3, starting transfers between devices, body(): down = lax.ppermute(down, 'tensor', down_pairs)  5.76 us
    ppermute x1, starting transfers between devices, body(): up = lax.ppermute(up[:tokens // 2], 'tensor', up_pairs)  5.6 us
    pallas_call x1, Pallas kernels, body(): pl.pallas_call(project_kernel, in_specs=[pl.BlockSpec(memory_space=pltpu....  3.19 us
    unnamed x14, local copies, waits for them, and re-layouts  3.17 us
  transfers between devices with their start and end apart: 9, of which 4 were waited for; matrix products, arithmetic and copies ran while one was open for 0% of the time, Pallas kernels for 6%

profile of v3, /device:TPU:30, one launch (start us, length us, event | category | flops | bytes accessed | tf_op | source)
XLA Modules:
  0.0 116.0 jit_solution(3086461361818956453)
XLA Ops:
  6.5 0.0 copy-start.6
  6.5 0.0 copy-start.5
  6.5 0.0 all-gather.2.cloned.1.call-start
  6.5 0.7 all-gather.2.cloned.1.call-update
  7.3 0.0 copy-start
  7.3 0.9 copy-done
  8.2 0.0 copy-start.3
  8.2 1.0 copy-done.3
  9.3 0.0 copy-start.1
  9.3 0.0 copy-start.4
  9.3 0.2 shard_map.73
  9.5 31.1 %all_to_all.10.x_ref = bf16[64,16,256]{2,1,0:T(8,128)(2,1)S(1)} all-to-all(bf16[64,16,256]{2,1,0:T(8,128)(2,1)S(1)} %shard_map.73), channel_id=1, replica_groups=mesh['seq'=64,'tensor'=8] {'seq'}, dimensions={0} | all-to-all | bytes 1048576 | tf_op jit(solution)/shard_map/all_to_all | solution.py:201
  40.6 0.0 copy-start.2
  40.6 1.2 %copy-done.2 = bf16[864,512]{1,0:T(8,128)(2,1)S(1)} copy-done((bf16[864,512]{1,0:T(8,128)(2,1)S(1)}, bf16[864,512]{1,0:T(8,128)(2,1)}, u32[]{:S(2)}) %copy-start.2) | copy-done | bytes 884760
  41.7 3.0 %shard_map.74 = bf16[64,16,128]{2,1,0:T(8,128)(2,1)S(1)} custom-call(bf16[64,16,256]{2,1,0:T(8,128)(2,1)S(1)} %all_to_all.10.x_ref, bf16[864,512]{1,0:T(8,128)(2,1)S(1)} %copy-done.2), custom_call_target="tpu_custom_call" | custom-call | tf_op jit(solution)/shard_map/pallas_call | solution.py:202
  44.7 18.5 %all_to_all.11.back_ref = bf16[64,16,128]{2,1,0:T(8,128)(2,1)S(1)} all-to-all(bf16[64,16,128]{2,1,0:T(8,128)(2,1)S(1)} %shard_map.74), channel_id=1, replica_groups=mesh['seq'=64,'tensor'=8] {'seq'}, dimensions={0} | all-to-all | bytes 524288 | tf_op jit(solution)/shard_map/all_to_all | solution.py:215
  63.2 0.0 copy-done.5
  63.2 0.0 copy-done.1
  63.2 0.0 copy-done.4
  63.2 0.2 shard_map.75.refs_0_
  63.3 4.7 %collective-permute-start = (bf16[256,512]{1,0:T(8,128)(2,1)S(1)}, bf16[256,512]{1,0:T(8,128)(2,1)S(1)}, u32[]{:S(2)}, u32[]{:S(2)}) collective-permute-start(bf16[256,512]{1,0:T(8,128)(2,1)S(1)} %shard_map.75.refs_0_), channel_id=1, source_target_pairs={{0,1},{1,2},{2,3},{3,4},{4,5},{5,6},{6,7},{7,0},{8,9},{9,10},{10,1... | collective-permute-start | bytes 786440 | tf_op jit(solution)/shard_map/ppermute | solution.py:224
  68.1 1.9 %collective-permute-start.1 = (bf16[256,512]{1,0:T(8,128)(2,1)S(1)}, bf16[256,512]{1,0:T(8,128)(2,1)S(1)}, u32[]{:S(2)}, u32[]{:S(2)}) collective-permute-start(bf16[256,512]{1,0:T(8,128)(2,1)S(1)} %shard_map.75.refs_0_), channel_id=1, source_target_pairs={{0,7},{1,0},{2,1},{3,2},{4,3},{5,4},{6,5},{7,6},{8,15},{9,8},{10,9... | collective-permute-start | bytes 786440 | tf_op jit(solution)/shard_map/ppermute | solution.py:225
  70.0 3.9 %collective-permute-done.refs_1_ = bf16[256,512]{1,0:T(8,128)(2,1)S(1)} collective-permute-done((bf16[256,512]{1,0:T(8,128)(2,1)S(1)}, bf16[256,512]{1,0:T(8,128)(2,1)S(1)}, u32[]{:S(2)}, u32[]{:S(2)}) %collective-permute-start) | collective-permute-done | bytes 262176 | tf_op jit(solution)/shard_map/ppermute | solution.py:224
  73.9 5.6 %collective-permute-start.2 = (bf16[256,512]{1,0:T(8,128)(2,1)S(1)}, bf16[256,512]{1,0:T(8,128)(2,1)S(1)}, u32[]{:S(2)}, u32[]{:S(2)}) collective-permute-start(bf16[256,512]{1,0:T(8,128)(2,1)S(1)} %collective-permute-done.refs_1_), channel_id=1, source_target_pairs={{0,1},{1,2},{2,3},{3,4},{4,5},{5,6},{6,7},{7,0},{8,9},{9,10},{10,1... | collective-permute-start | bytes 786440 | tf_op jit(solution)/shard_map/ppermute | solution.py:224
  79.5 0.0 collective-permute-done.1.refs_2_
  79.5 1.9 %collective-permute-start.3 = (bf16[256,512]{1,0:T(8,128)(2,1)S(1)}, bf16[256,512]{1,0:T(8,128)(2,1)S(1)}, u32[]{:S(2)}, u32[]{:S(2)}) collective-permute-start(bf16[256,512]{1,0:T(8,128)(2,1)S(1)} %collective-permute-done.1.refs_2_), channel_id=1, source_target_pairs={{0,7},{1,0},{2,1},{3,2},{4,3},{5,4},{6,5},{7,6},{8,15},{9,8},{10,9... | collective-permute-start | bytes 786440 | tf_op jit(solution)/shard_map/ppermute | solution.py:225
  81.4 3.2 %collective-permute-done.2.refs_3_ = bf16[256,512]{1,0:T(8,128)(2,1)S(1)} collective-permute-done((bf16[256,512]{1,0:T(8,128)(2,1)S(1)}, bf16[256,512]{1,0:T(8,128)(2,1)S(1)}, u32[]{:S(2)}, u32[]{:S(2)}) %collective-permute-start.2) | collective-permute-done | bytes 262176 | tf_op jit(solution)/shard_map/ppermute | solution.py:224
  84.6 5.6 %collective-permute-start.4 = (bf16[256,512]{1,0:T(8,128)(2,1)S(1)}, bf16[256,512]{1,0:T(8,128)(2,1)S(1)}, u32[]{:S(2)}, u32[]{:S(2)}) collective-permute-start(bf16[256,512]{1,0:T(8,128)(2,1)S(1)} %collective-permute-done.2.refs_3_), channel_id=1, source_target_pairs={{0,1},{1,2},{2,3},{3,4},{4,5},{5,6},{6,7},{7,0},{8,9},{9,10},{10,1... | collective-permute-start | bytes 786440 | tf_op jit(solution)/shard_map/ppermute | solution.py:224
  90.2 0.0 collective-permute-done.3.refs_4_
  90.2 1.9 %collective-permute-start.5 = (bf16[256,512]{1,0:T(8,128)(2,1)S(1)}, bf16[256,512]{1,0:T(8,128)(2,1)S(1)}, u32[]{:S(2)}, u32[]{:S(2)}) collective-permute-start(bf16[256,512]{1,0:T(8,128)(2,1)S(1)} %collective-permute-done.3.refs_4_), channel_id=1, source_target_pairs={{0,7},{1,0},{2,1},{3,2},{4,3},{5,4},{6,5},{7,6},{8,15},{9,8},{10,9... | collective-permute-start | bytes 786440 | tf_op jit(solution)/shard_map/ppermute | solution.py:225
  92.1 2.3 %collective-permute-done.4.refs_5_ = bf16[256,512]{1,0:T(8,128)(2,1)S(1)} collective-permute-done((bf16[256,512]{1,0:T(8,128)(2,1)S(1)}, bf16[256,512]{1,0:T(8,128)(2,1)S(1)}, u32[]{:S(2)}, u32[]{:S(2)}) %collective-permute-start.4) | collective-permute-done | bytes 262176 | tf_op jit(solution)/shard_map/ppermute | solution.py:224
  94.5 5.6 %collective-permute-start.6 = (bf16[128,512]{1,0:T(8,128)(2,1)S(1)}, bf16[128,512]{1,0:T(8,128)(2,1)S(1)}, u32[]{:S(2)}, u32[]{:S(2)}) collective-permute-start(bf16[128,512]{1,0:T(8,128)(2,1)S(1)} %slice.8), channel_id=1, source_target_pairs={{0,1},{1,2},{2,3},{3,4},{4,5},{5,6},{6,7},{7,0},{8,9},{9,10},{10,1... | collective-permute-start | bytes 393224 | tf_op jit(solution)/shard_map/ppermute | solution.py:228
  100.1 0.0 collective-permute-done.5.refs_6_
  100.1 1.9 %collective-permute-start.7 = (bf16[128,512]{1,0:T(8,128)(2,1)S(1)}, bf16[128,512]{1,0:T(8,128)(2,1)S(1)}, u32[]{:S(2)}, u32[]{:S(2)}) collective-permute-start(bf16[128,512]{1,0:T(8,128)(2,1)S(1)} %slice.9), channel_id=1, source_target_pairs={{0,7},{1,0},{2,1},{3,2},{4,3},{5,4},{6,5},{7,6},{8,15},{9,8},{10,9... | collective-permute-start | bytes 393224 | tf_op jit(solution)/shard_map/ppermute | solution.py:229
  102.0 0.0 copy-done.6
  102.1 0.0 all-gather.2.cloned.1.call-done.refs_7_
  102.1 3.2 %shard_map.76 = (f32[256,512]{1,0:T(8,128)S(1)}, bf16[512,512]{1,0:T(8,128)(2,1)S(1)}) custom-call(s32[8]{0:T(128)S(1)} %and_select_fusion.index_ref, bf16[256,512]{1,0:T(8,128)(2,1)S(1)} %shard_map.75.refs_0_, bf16[256,512]{1,0:T(8,128)(2,1)S(1)} %collective-permute-done.refs_1_, bf16[256,512]{1,0:T(8,128)(2,1)S(1)} %collective-permute-done.1.refs_2_, ...), custom_call_target="tpu_custom_call" | custom-call | tf_op jit(solution)/shard_map/pallas_call | solution.py:232
  105.3 0.0 collective-permute-done.6.up_ref
  105.3 2.9 %collective-permute-done.7.down_ref = bf16[128,512]{1,0:T(8,128)(2,1)S(1)} collective-permute-done((bf16[128,512]{1,0:T(8,128)(2,1)S(1)}, bf16[128,512]{1,0:T(8,128)(2,1)S(1)}, u32[]{:S(2)}, u32[]{:S(2)}) %collective-permute-start.7) | collective-permute-done | bytes 131104 | tf_op jit(solution)/shard_map/ppermute | solution.py:229
  108.2 1.0 shard_map.77
  (3 shorter events, 0.0 us)
Async XLA Ops:
  6.5 95.5 %copy-start.6 = (s32[8]{0:T(128)S(1)}, s32[8]{0:T(128)}, u32[]{:S(2)}) copy-start(s32[8]{0:T(128)} %constant.24.clone) | copy-start | bytes 100
  6.5 56.6 %copy-start.5 = (f32[512]{0:T(512)S(1)}, f32[512]{0:T(512)}, u32[]{:S(2)}) copy-start(f32[512]{0:T(512)} %param.10) | copy-start | bytes 6148
  6.5 95.5 %all-gather.2.cloned.1.call-start = ((), (), s32[]{:S(2)}) async-start(), calls=%async_computation.2 | async-start | bytes 4259840 | tf_op jit(solution)/shard_map/all_gather | solution.py:190
  7.3 1.0 copy-start
  8.2 1.0 copy-start.3
  9.3 53.9 %copy-start.1 = (bf16[256,512]{1,0:T(8,128)(2,1)S(1)}, bf16[256,512]{1,0:T(8,128)(2,1)}, u32[]{:S(2)}) copy-start(bf16[256,512]{1,0:T(8,128)(2,1)} %signal_ref.3) | copy-start | bytes 786436
  9.3 53.9 %copy-start.4 = (bf16[256,512]{1,0:T(8,128)(2,1)S(1)}, bf16[256,512]{1,0:T(8,128)(2,1)}, u32[]{:S(2)}) copy-start(bf16[256,512]{1,0:T(8,128)(2,1)} %gating_ref.1) | copy-start | bytes 786436
  40.6 1.2 %copy-start.2 = (bf16[864,512]{1,0:T(8,128)(2,1)S(1)}, bf16[864,512]{1,0:T(8,128)(2,1)}, u32[]{:S(2)}) copy-start(bf16[864,512]{1,0:T(8,128)(2,1)} %constant.23.clone.table_ref) | copy-start | bytes 2654212
  63.3 10.6 %collective-permute-start = (bf16[256,512]{1,0:T(8,128)(2,1)S(1)}, bf16[256,512]{1,0:T(8,128)(2,1)S(1)}, u32[]{:S(2)}, u32[]{:S(2)}) collective-permute-start(bf16[256,512]{1,0:T(8,128)(2,1)S(1)} %shard_map.75.refs_0_), channel_id=1, source_target_pairs={{0,1},{1,2},{2,3},{3,4},{4,5},{5,6},{6,7},{7,0},{8,9},{9,10},{10,1... | collective-permute-start | bytes 786440 | tf_op jit(solution)/shard_map/ppermute | solution.py:224
  68.1 11.4 %collective-permute-start.1 = (bf16[256,512]{1,0:T(8,128)(2,1)S(1)}, bf16[256,512]{1,0:T(8,128)(2,1)S(1)}, u32[]{:S(2)}, u32[]{:S(2)}) collective-permute-start(bf16[256,512]{1,0:T(8,128)(2,1)S(1)} %shard_map.75.refs_0_), channel_id=1, source_target_pairs={{0,7},{1,0},{2,1},{3,2},{4,3},{5,4},{6,5},{7,6},{8,15},{9,8},{10,9... | collective-permute-start | bytes 786440 | tf_op jit(solution)/shard_map/ppermute | solution.py:225
  73.9 10.7 %collective-permute-start.2 = (bf16[256,512]{1,0:T(8,128)(2,1)S(1)}, bf16[256,512]{1,0:T(8,128)(2,1)S(1)}, u32[]{:S(2)}, u32[]{:S(2)}) collective-permute-start(bf16[256,512]{1,0:T(8,128)(2,1)S(1)} %collective-permute-done.refs_1_), channel_id=1, source_target_pairs={{0,1},{1,2},{2,3},{3,4},{4,5},{5,6},{6,7},{7,0},{8,9},{9,10},{10,1... | collective-permute-start | bytes 786440 | tf_op jit(solution)/shard_map/ppermute | solution.py:224
  79.5 10.7 %collective-permute-start.3 = (bf16[256,512]{1,0:T(8,128)(2,1)S(1)}, bf16[256,512]{1,0:T(8,128)(2,1)S(1)}, u32[]{:S(2)}, u32[]{:S(2)}) collective-permute-start(bf16[256,512]{1,0:T(8,128)(2,1)S(1)} %collective-permute-done.1.refs_2_), channel_id=1, source_target_pairs={{0,7},{1,0},{2,1},{3,2},{4,3},{5,4},{6,5},{7,6},{8,15},{9,8},{10,9... | collective-permute-start | bytes 786440 | tf_op jit(solution)/shard_map/ppermute | solution.py:225
  84.6 9.9 %collective-permute-start.4 = (bf16[256,512]{1,0:T(8,128)(2,1)S(1)}, bf16[256,512]{1,0:T(8,128)(2,1)S(1)}, u32[]{:S(2)}, u32[]{:S(2)}) collective-permute-start(bf16[256,512]{1,0:T(8,128)(2,1)S(1)} %collective-permute-done.2.refs_3_), channel_id=1, source_target_pairs={{0,1},{1,2},{2,3},{3,4},{4,5},{5,6},{6,7},{7,0},{8,9},{9,10},{10,1... | collective-permute-start | bytes 786440 | tf_op jit(solution)/shard_map/ppermute | solution.py:224
  90.2 9.9 %collective-permute-start.5 = (bf16[256,512]{1,0:T(8,128)(2,1)S(1)}, bf16[256,512]{1,0:T(8,128)(2,1)S(1)}, u32[]{:S(2)}, u32[]{:S(2)}) collective-permute-start(bf16[256,512]{1,0:T(8,128)(2,1)S(1)} %collective-permute-done.3.refs_4_), channel_id=1, source_target_pairs={{0,7},{1,0},{2,1},{3,2},{4,3},{5,4},{6,5},{7,6},{8,15},{9,8},{10,9... | collective-permute-start | bytes 786440 | tf_op jit(solution)/shard_map/ppermute | solution.py:225
  94.5 10.8 %collective-permute-start.6 = (bf16[128,512]{1,0:T(8,128)(2,1)S(1)}, bf16[128,512]{1,0:T(8,128)(2,1)S(1)}, u32[]{:S(2)}, u32[]{:S(2)}) collective-permute-start(bf16[128,512]{1,0:T(8,128)(2,1)S(1)} %slice.8), channel_id=1, source_target_pairs={{0,1},{1,2},{2,3},{3,4},{4,5},{5,6},{6,7},{7,0},{8,9},{9,10},{10,1... | collective-permute-start | bytes 393224 | tf_op jit(solution)/shard_map/ppermute | solution.py:228
  100.1 8.1 %collective-permute-start.7 = (bf16[128,512]{1,0:T(8,128)(2,1)S(1)}, bf16[128,512]{1,0:T(8,128)(2,1)S(1)}, u32[]{:S(2)}, u32[]{:S(2)}) collective-permute-start(bf16[128,512]{1,0:T(8,128)(2,1)S(1)} %slice.9), channel_id=1, source_target_pairs={{0,7},{1,0},{2,1},{3,2},{4,3},{5,4},{6,5},{7,6},{8,15},{9,8},{10,9... | collective-permute-start | bytes 393224 | tf_op jit(solution)/shard_map/ppermute | solution.py:229
Sparse Core Ops, SparseCore 0:
  10.7 89.3 all-gather.1

commit v4 on v3

--- a/solution.py
+++ b/solution.py
@@ -218,15 +218,22 @@
     )(returned, signal, gating, skip_gain.reshape(1, channels))
     up_pairs = [(t, (t + 1) % ring) for t in range(ring)]
     down_pairs = [(t, (t - 1) % ring) for t in range(ring)]
+    up_two = [(t, (t + 2) % ring) for t in range(ring)]
+    down_two = [(t, (t - 2) % ring) for t in range(ring)]
     pieces, offsets = [gated], [0]
     up = down = gated
-    for n in range(1, ring // 2):
+    for n in range(1, ring // 2 - 1):
         up = lax.ppermute(up, "tensor", up_pairs)
         down = lax.ppermute(down, "tensor", down_pairs)
         pieces += [up, down]
         offsets += [-n, n]
-    up = lax.ppermute(up[: tokens // 2], "tensor", up_pairs)
-    down = lax.ppermute(down[tokens // 2 :], "tensor", down_pairs)
+    up_next = lax.ppermute(up, "tensor", up_pairs)
+    down_next = lax.ppermute(down, "tensor", down_pairs)
+    up_far = lax.ppermute(up[: tokens // 2], "tensor", up_two)
+    down_far = lax.ppermute(down[tokens // 2 :], "tensor", down_two)
+    pieces += [up_next, down_next]
+    offsets += [1 - ring // 2, ring // 2 - 1]
+    up, down = up_far, down_far
     offsets.append(ring // 2)
     index = (lax.axis_index("tensor") + jnp.asarray(offsets, jnp.int32)) % ring
     total, last_weight = pl.pallas_call(

time: 117 us -> 117 us (level)
  the two profiles are of different devices: /device:TPU:30 before, /device:TPU:22 now
where the time goes in v4:
time: 117 us; the launch traced here: 116 us
  blocking collectives  49.5 us (42%)
  starting transfers between devices  28.3 us (24%)
  waiting for transfers between devices  14.1 us (12%)
  between operations  13.6 us (12%)
  Pallas kernels  7.52 us (6%)
  local copies, waits for them, and re-layouts  3.19 us (3%)
    all_to_all x1, blocking collectives, body(): lax.all_to_all(packed, 'seq', split_axis=0, concat_axis=0, tiled=True)  31.1 us
    all_to_all x1, blocking collectives, body(): lax.all_to_all(convolved, 'seq', split_axis=0, concat_axis=0, tiled=True)  18.4 us
    ppermute x1, starting transfers between devices, body(): up_far = lax.ppermute(up[:tokens // 2], 'tensor', up_two)  7.79 us
    ppermute x2, waiting for transfers between devices, body(): up = lax.ppermute(up, 'tensor', up_pairs)  7.58 us
    ppermute x2, starting transfers between devices, body(): up = lax.ppermute(up, 'tensor', up_pairs)  7.38 us
    ppermute x1, starting transfers between devices, body(): up_next = lax.ppermute(up, 'tensor', up_pairs)  5.07 us
    ppermute x1, waiting for transfers between devices, body(): down_far = lax.ppermute(down[tokens // 2:], 'tensor', down_two)  4.8 us
    ppermute x2, starting transfers between devices, body(): down = lax.ppermute(down, 'tensor', down_pairs)  4.23 us
  transfers between devices with their start and end apart: 9, of which 5 were waited for; matrix products, arithmetic and copies ran while one was open for 0% of the time, Pallas kernels for 6%

profile of v4, /device:TPU:22, one launch (start us, length us, event | category | flops | bytes accessed | tf_op | source)
XLA Modules:
  0.0 116.2 jit_solution(5909555632094750274)
XLA Ops:
  6.5 0.0 copy-start.6
  6.5 0.0 copy-start.5
  6.5 0.0 all-gather.2.cloned.1.call-start
  6.5 0.7 all-gather.2.cloned.1.call-update
  7.3 0.0 copy-start
  7.3 0.9 copy-done
  8.2 0.0 copy-start.3
  8.2 1.0 copy-done.3
  9.3 0.0 copy-start.1
  9.3 0.0 copy-start.4
  9.3 0.2 shard_map.73
  9.5 31.1 %all_to_all.10.x_ref = bf16[64,16,256]{2,1,0:T(8,128)(2,1)S(1)} all-to-all(bf16[64,16,256]{2,1,0:T(8,128)(2,1)S(1)} %shard_map.73), channel_id=1, replica_groups=mesh['seq'=64,'tensor'=8] {'seq'}, dimensions={0} | all-to-all | bytes 1048576 | tf_op jit(solution)/shard_map/all_to_all | solution.py:201
  40.6 0.0 copy-start.2
  40.6 1.2 %copy-done.2 = bf16[864,512]{1,0:T(8,128)(2,1)S(1)} copy-done((bf16[864,512]{1,0:T(8,128)(2,1)S(1)}, bf16[864,512]{1,0:T(8,128)(2,1)}, u32[]{:S(2)}) %copy-start.2) | copy-done | bytes 884760
  41.7 3.0 %shard_map.74 = bf16[64,16,128]{2,1,0:T(8,128)(2,1)S(1)} custom-call(bf16[64,16,256]{2,1,0:T(8,128)(2,1)S(1)} %all_to_all.10.x_ref, bf16[864,512]{1,0:T(8,128)(2,1)S(1)} %copy-done.2), custom_call_target="tpu_custom_call" | custom-call | tf_op jit(solution)/shard_map/pallas_call | solution.py:202
  44.7 18.4 %all_to_all.11.back_ref = bf16[64,16,128]{2,1,0:T(8,128)(2,1)S(1)} all-to-all(bf16[64,16,128]{2,1,0:T(8,128)(2,1)S(1)} %shard_map.74), channel_id=1, replica_groups=mesh['seq'=64,'tensor'=8] {'seq'}, dimensions={0} | all-to-all | bytes 524288 | tf_op jit(solution)/shard_map/all_to_all | solution.py:215
  63.1 0.0 copy-done.5
  63.1 0.0 copy-done.1
  63.1 0.0 copy-done.4
  63.1 0.2 shard_map.75.refs_0_
  63.3 3.5 %collective-permute-start = (bf16[256,512]{1,0:T(8,128)(2,1)S(1)}, bf16[256,512]{1,0:T(8,128)(2,1)S(1)}, u32[]{:S(2)}, u32[]{:S(2)}) collective-permute-start(bf16[256,512]{1,0:T(8,128)(2,1)S(1)} %shard_map.75.refs_0_), channel_id=1, source_target_pairs={{0,1},{1,2},{2,3},{3,4},{4,5},{5,6},{6,7},{7,0},{8,9},{9,10},{10,1... | collective-permute-start | bytes 786440 | tf_op jit(solution)/shard_map/ppermute | solution.py:226
  66.8 2.3 %collective-permute-start.1 = (bf16[256,512]{1,0:T(8,128)(2,1)S(1)}, bf16[256,512]{1,0:T(8,128)(2,1)S(1)}, u32[]{:S(2)}, u32[]{:S(2)}) collective-permute-start(bf16[256,512]{1,0:T(8,128)(2,1)S(1)} %shard_map.75.refs_0_), channel_id=1, source_target_pairs={{0,7},{1,0},{2,1},{3,2},{4,3},{5,4},{6,5},{7,6},{8,15},{9,8},{10,9... | collective-permute-start | bytes 786440 | tf_op jit(solution)/shard_map/ppermute | solution.py:227
  69.1 4.4 %collective-permute-done.refs_1_ = bf16[256,512]{1,0:T(8,128)(2,1)S(1)} collective-permute-done((bf16[256,512]{1,0:T(8,128)(2,1)S(1)}, bf16[256,512]{1,0:T(8,128)(2,1)S(1)}, u32[]{:S(2)}, u32[]{:S(2)}) %collective-permute-start) | collective-permute-done | bytes 262176 | tf_op jit(solution)/shard_map/ppermute | solution.py:226
  73.5 3.9 %collective-permute-start.2 = (bf16[256,512]{1,0:T(8,128)(2,1)S(1)}, bf16[256,512]{1,0:T(8,128)(2,1)S(1)}, u32[]{:S(2)}, u32[]{:S(2)}) collective-permute-start(bf16[256,512]{1,0:T(8,128)(2,1)S(1)} %collective-permute-done.refs_1_), channel_id=1, source_target_pairs={{0,1},{1,2},{2,3},{3,4},{4,5},{5,6},{6,7},{7,0},{8,9},{9,10},{10,1... | collective-permute-start | bytes 786440 | tf_op jit(solution)/shard_map/ppermute | solution.py:226
  77.4 0.5 collective-permute-done.1.refs_2_
  77.9 1.9 %collective-permute-start.3 = (bf16[256,512]{1,0:T(8,128)(2,1)S(1)}, bf16[256,512]{1,0:T(8,128)(2,1)S(1)}, u32[]{:S(2)}, u32[]{:S(2)}) collective-permute-start(bf16[256,512]{1,0:T(8,128)(2,1)S(1)} %collective-permute-done.1.refs_2_), channel_id=1, source_target_pairs={{0,7},{1,0},{2,1},{3,2},{4,3},{5,4},{6,5},{7,6},{8,15},{9,8},{10,9... | collective-permute-start | bytes 786440 | tf_op jit(solution)/shard_map/ppermute | solution.py:227
  79.8 3.2 %collective-permute-done.2.refs_3_ = bf16[256,512]{1,0:T(8,128)(2,1)S(1)} collective-permute-done((bf16[256,512]{1,0:T(8,128)(2,1)S(1)}, bf16[256,512]{1,0:T(8,128)(2,1)S(1)}, u32[]{:S(2)}, u32[]{:S(2)}) %collective-permute-start.2) | collective-permute-done | bytes 262176 | tf_op jit(solution)/shard_map/ppermute | solution.py:226
  83.0 5.1 %collective-permute-start.4 = (bf16[256,512]{1,0:T(8,128)(2,1)S(1)}, bf16[256,512]{1,0:T(8,128)(2,1)S(1)}, u32[]{:S(2)}, u32[]{:S(2)}) collective-permute-start(bf16[256,512]{1,0:T(8,128)(2,1)S(1)} %collective-permute-done.2.refs_3_), channel_id=1, source_target_pairs={{0,1},{1,2},{2,3},{3,4},{4,5},{5,6},{6,7},{7,0},{8,9},{9,10},{10,1... | collective-permute-start | bytes 786440 | tf_op jit(solution)/shard_map/ppermute | solution.py:230
  88.1 0.5 collective-permute-done.3.refs_4_
  88.6 1.9 %collective-permute-start.5 = (bf16[256,512]{1,0:T(8,128)(2,1)S(1)}, bf16[256,512]{1,0:T(8,128)(2,1)S(1)}, u32[]{:S(2)}, u32[]{:S(2)}) collective-permute-start(bf16[256,512]{1,0:T(8,128)(2,1)S(1)} %collective-permute-done.3.refs_4_), channel_id=1, source_target_pairs={{0,7},{1,0},{2,1},{3,2},{4,3},{5,4},{6,5},{7,6},{8,15},{9,8},{10,9... | collective-permute-start | bytes 786440 | tf_op jit(solution)/shard_map/ppermute | solution.py:231
  90.5 7.8 %collective-permute-start.6 = (bf16[128,512]{1,0:T(8,128)(2,1)S(1)}, bf16[128,512]{1,0:T(8,128)(2,1)S(1)}, u32[]{:S(2)}, u32[]{:S(2)}) collective-permute-start(bf16[128,512]{1,0:T(8,128)(2,1)S(1)} %slice.8), channel_id=1, source_target_pairs={{0,2},{1,3},{2,4},{3,5},{4,6},{5,7},{6,0},{7,1},{8,10},{9,11},{10,... | collective-permute-start | bytes 393224 | tf_op jit(solution)/shard_map/ppermute | solution.py:232
  98.3 1.9 %collective-permute-start.7 = (bf16[128,512]{1,0:T(8,128)(2,1)S(1)}, bf16[128,512]{1,0:T(8,128)(2,1)S(1)}, u32[]{:S(2)}, u32[]{:S(2)}) collective-permute-start(bf16[128,512]{1,0:T(8,128)(2,1)S(1)} %slice.9), channel_id=1, source_target_pairs={{0,6},{1,7},{2,0},{3,1},{4,2},{5,3},{6,4},{7,5},{8,14},{9,15},{10,... | collective-permute-start | bytes 393224 | tf_op jit(solution)/shard_map/ppermute | solution.py:233
  100.2 0.0 copy-done.6
  100.3 0.0 collective-permute-done.4.refs_5_
  100.3 0.0 collective-permute-done.5.refs_6_
  100.3 0.0 all-gather.2.cloned.1.call-done.refs_7_
  100.3 3.2 %shard_map.76 = (f32[256,512]{1,0:T(8,128)S(1)}, bf16[512,512]{1,0:T(8,128)(2,1)S(1)}) custom-call(s32[8]{0:T(128)S(1)} %and_select_fusion.index_ref, bf16[256,512]{1,0:T(8,128)(2,1)S(1)} %shard_map.75.refs_0_, bf16[256,512]{1,0:T(8,128)(2,1)S(1)} %collective-permute-done.refs_1_, bf16[256,512]{1,0:T(8,128)(2,1)S(1)} %collective-permute-done.1.refs_2_, ...), custom_call_target="tpu_custom_call" | custom-call | tf_op jit(solution)/shard_map/pallas_call | solution.py:239
  103.5 0.0 collective-permute-done.6.up_ref
  103.5 4.8 %collective-permute-done.7.down_ref = bf16[128,512]{1,0:T(8,128)(2,1)S(1)} collective-permute-done((bf16[128,512]{1,0:T(8,128)(2,1)S(1)}, bf16[128,512]{1,0:T(8,128)(2,1)S(1)}, u32[]{:S(2)}, u32[]{:S(2)}) %collective-permute-start.7) | collective-permute-done | bytes 131104 | tf_op jit(solution)/shard_map/ppermute | solution.py:233
  108.3 1.0 shard_map.77
  (3 shorter events, 0.0 us)
Async XLA Ops:
  6.5 93.7 %copy-start.6 = (s32[8]{0:T(128)S(1)}, s32[8]{0:T(128)}, u32[]{:S(2)}) copy-start(s32[8]{0:T(128)} %constant.24.clone) | copy-start | bytes 100
  6.5 56.6 %copy-start.5 = (f32[512]{0:T(512)S(1)}, f32[512]{0:T(512)}, u32[]{:S(2)}) copy-start(f32[512]{0:T(512)} %param.10) | copy-start | bytes 6148
  6.5 93.8 %all-gather.2.cloned.1.call-start = ((), (), s32[]{:S(2)}) async-start(), calls=%async_computation.2 | async-start | bytes 4259840 | tf_op jit(solution)/shard_map/all_gather | solution.py:190
  7.3 1.0 copy-start
  8.2 1.0 copy-start.3
  9.3 53.9 %copy-start.1 = (bf16[256,512]{1,0:T(8,128)(2,1)S(1)}, bf16[256,512]{1,0:T(8,128)(2,1)}, u32[]{:S(2)}) copy-start(bf16[256,512]{1,0:T(8,128)(2,1)} %signal_ref.3) | copy-start | bytes 786436
  9.3 53.9 %copy-start.4 = (bf16[256,512]{1,0:T(8,128)(2,1)S(1)}, bf16[256,512]{1,0:T(8,128)(2,1)}, u32[]{:S(2)}) copy-start(bf16[256,512]{1,0:T(8,128)(2,1)} %gating_ref.1) | copy-start | bytes 786436
  40.6 1.2 %copy-start.2 = (bf16[864,512]{1,0:T(8,128)(2,1)S(1)}, bf16[864,512]{1,0:T(8,128)(2,1)}, u32[]{:S(2)}) copy-start(bf16[864,512]{1,0:T(8,128)(2,1)} %constant.23.clone.table_ref) | copy-start | bytes 2654212
  63.3 10.2 %collective-permute-start = (bf16[256,512]{1,0:T(8,128)(2,1)S(1)}, bf16[256,512]{1,0:T(8,128)(2,1)S(1)}, u32[]{:S(2)}, u32[]{:S(2)}) collective-permute-start(bf16[256,512]{1,0:T(8,128)(2,1)S(1)} %shard_map.75.refs_0_), channel_id=1, source_target_pairs={{0,1},{1,2},{2,3},{3,4},{4,5},{5,6},{6,7},{7,0},{8,9},{9,10},{10,1... | collective-permute-start | bytes 786440 | tf_op jit(solution)/shard_map/ppermute | solution.py:226
  66.8 11.0 %collective-permute-start.1 = (bf16[256,512]{1,0:T(8,128)(2,1)S(1)}, bf16[256,512]{1,0:T(8,128)(2,1)S(1)}, u32[]{:S(2)}, u32[]{:S(2)}) collective-permute-start(bf16[256,512]{1,0:T(8,128)(2,1)S(1)} %shard_map.75.refs_0_), channel_id=1, source_target_pairs={{0,7},{1,0},{2,1},{3,2},{4,3},{5,4},{6,5},{7,6},{8,15},{9,8},{10,9... | collective-permute-start | bytes 786440 | tf_op jit(solution)/shard_map/ppermute | solution.py:227
  73.5 9.5 %collective-permute-start.2 = (bf16[256,512]{1,0:T(8,128)(2,1)S(1)}, bf16[256,512]{1,0:T(8,128)(2,1)S(1)}, u32[]{:S(2)}, u32[]{:S(2)}) collective-permute-start(bf16[256,512]{1,0:T(8,128)(2,1)S(1)} %collective-permute-done.refs_1_), channel_id=1, source_target_pairs={{0,1},{1,2},{2,3},{3,4},{4,5},{5,6},{6,7},{7,0},{8,9},{9,10},{10,1... | collective-permute-start | bytes 786440 | tf_op jit(solution)/shard_map/ppermute | solution.py:226
  77.9 10.7 %collective-permute-start.3 = (bf16[256,512]{1,0:T(8,128)(2,1)S(1)}, bf16[256,512]{1,0:T(8,128)(2,1)S(1)}, u32[]{:S(2)}, u32[]{:S(2)}) collective-permute-start(bf16[256,512]{1,0:T(8,128)(2,1)S(1)} %collective-permute-done.1.refs_2_), channel_id=1, source_target_pairs={{0,7},{1,0},{2,1},{3,2},{4,3},{5,4},{6,5},{7,6},{8,15},{9,8},{10,9... | collective-permute-start | bytes 786440 | tf_op jit(solution)/shard_map/ppermute | solution.py:227
  83.0 17.3 %collective-permute-start.4 = (bf16[256,512]{1,0:T(8,128)(2,1)S(1)}, bf16[256,512]{1,0:T(8,128)(2,1)S(1)}, u32[]{:S(2)}, u32[]{:S(2)}) collective-permute-start(bf16[256,512]{1,0:T(8,128)(2,1)S(1)} %collective-permute-done.2.refs_3_), channel_id=1, source_target_pairs={{0,1},{1,2},{2,3},{3,4},{4,5},{5,6},{6,7},{7,0},{8,9},{9,10},{10,1... | collective-permute-start | bytes 786440 | tf_op jit(solution)/shard_map/ppermute | solution.py:230
  88.6 11.7 %collective-permute-start.5 = (bf16[256,512]{1,0:T(8,128)(2,1)S(1)}, bf16[256,512]{1,0:T(8,128)(2,1)S(1)}, u32[]{:S(2)}, u32[]{:S(2)}) collective-permute-start(bf16[256,512]{1,0:T(8,128)(2,1)S(1)} %collective-permute-done.3.refs_4_), channel_id=1, source_target_pairs={{0,7},{1,0},{2,1},{3,2},{4,3},{5,4},{6,5},{7,6},{8,15},{9,8},{10,9... | collective-permute-start | bytes 786440 | tf_op jit(solution)/shard_map/ppermute | solution.py:231
  90.5 13.0 %collective-permute-start.6 = (bf16[128,512]{1,0:T(8,128)(2,1)S(1)}, bf16[128,512]{1,0:T(8,128)(2,1)S(1)}, u32[]{:S(2)}, u32[]{:S(2)}) collective-permute-start(bf16[128,512]{1,0:T(8,128)(2,1)S(1)} %slice.8), channel_id=1, source_target_pairs={{0,2},{1,3},{2,4},{3,5},{4,6},{5,7},{6,0},{7,1},{8,10},{9,11},{10,... | collective-permute-start | bytes 393224 | tf_op jit(solution)/shard_map/ppermute | solution.py:232
  98.3 10.0 %collective-permute-start.7 = (bf16[128,512]{1,0:T(8,128)(2,1)S(1)}, bf16[128,512]{1,0:T(8,128)(2,1)S(1)}, u32[]{:S(2)}, u32[]{:S(2)}) collective-permute-start(bf16[128,512]{1,0:T(8,128)(2,1)S(1)} %slice.9), channel_id=1, source_target_pairs={{0,6},{1,7},{2,0},{3,1},{4,2},{5,3},{6,4},{7,5},{8,14},{9,15},{10,... | collective-permute-start | bytes 393224 | tf_op jit(solution)/shard_map/ppermute | solution.py:233
Sparse Core Ops, SparseCore 0:
  10.7 89.1 all-gather.1

commit v5 on v2

--- a/solution.py
+++ b/solution.py
@@ -220,15 +220,22 @@
     )(returned, signal, gating, skip_gain.reshape(1, channels))
     up_pairs = [(t, (t + 1) % ring) for t in range(ring)]
     down_pairs = [(t, (t - 1) % ring) for t in range(ring)]
+    up_two = [(t, (t + 2) % ring) for t in range(ring)]
+    down_two = [(t, (t - 2) % ring) for t in range(ring)]
     pieces, offsets = [gated], [0]
     up = down = gated
-    for n in range(1, ring // 2):
+    for n in range(1, ring // 2 - 1):
         up = lax.ppermute(up, "tensor", up_pairs)
         down = lax.ppermute(down, "tensor", down_pairs)
         pieces += [up, down]
         offsets += [-n, n]
-    up = lax.ppermute(up[: tokens // 2], "tensor", up_pairs)
-    down = lax.ppermute(down[tokens // 2 :], "tensor", down_pairs)
+    up_next = lax.ppermute(up, "tensor", up_pairs)
+    down_next = lax.ppermute(down, "tensor", down_pairs)
+    up_far = lax.ppermute(up[: tokens // 2], "tensor", up_two)
+    down_far = lax.ppermute(down[tokens // 2 :], "tensor", down_two)
+    pieces += [up_next, down_next]
+    offsets += [1 - ring // 2, ring // 2 - 1]
+    up, down = up_far, down_far
     offsets.append(ring // 2)
     index = (lax.axis_index("tensor") + jnp.asarray(offsets, jnp.int32)) % ring
     total, last_weight = pl.pallas_call(

time: 117 us -> 118 us (level)
  the two profiles are of different devices: /device:TPU:24 before, /device:TPU:16 now
where the time goes in v5:
time: 118 us; the launch traced here: 117 us
  blocking collectives  49.4 us (42%)
  starting transfers between devices  28.2 us (24%)
  waiting for transfers between devices  14.2 us (12%)
  between operations  13.6 us (12%)
  Pallas kernels  8.53 us (7%)
  local copies, waits for them, and re-layouts  3.19 us (3%)
    all_to_all x1, blocking collectives, body(): lax.all_to_all(packed, 'seq', split_axis=0, concat_axis=0, tiled=True)  31.4 us
    all_to_all x1, blocking collectives, body(): lax.all_to_all(convolved, 'seq', split_axis=0, concat_axis=0, tiled=True)  18 us
    ppermute x1, starting transfers between devices, body(): up_far = lax.ppermute(up[:tokens // 2], 'tensor', up_two)  7.79 us
    ppermute x2, waiting for transfers between devices, body(): up = lax.ppermute(up, 'tensor', up_pairs)  7.64 us
    ppermute x2, starting transfers between devices, body(): up = lax.ppermute(up, 'tensor', up_pairs)  7.24 us
    ppermute x1, starting transfers between devices, body(): up_next = lax.ppermute(up, 'tensor', up_pairs)  5 us
    ppermute x1, waiting for transfers between devices, body(): down_far = lax.ppermute(down[tokens // 2:], 'tensor', down_two)  4.8 us
    ppermute x2, starting transfers between devices, body(): down = lax.ppermute(down, 'tensor', down_pairs)  4.3 us
  transfers between devices with their start and end apart: 9, of which 5 were waited for; matrix products, arithmetic and copies ran while one was open for 0% of the time, Pallas kernels for 6%

profile of v5, /device:TPU:16, one launch (start us, length us, event | category | flops | bytes accessed | tf_op | source)
XLA Modules:
  0.0 117.0 jit_solution(7362651562917613923)
XLA Ops:
  6.5 0.0 copy-start.6
  6.5 0.0 copy-start.5
  6.5 0.0 all-gather.2.cloned.1.call-start
  6.5 0.7 all-gather.2.cloned.1.call-update
  7.3 0.0 copy-start
  7.3 0.9 copy-done
  8.2 0.0 copy-start.3
  8.2 1.0 copy-done.3
  9.3 0.0 copy-start.1
  9.3 0.0 copy-start.4
  9.3 0.2 shard_map.73
  9.5 31.4 %all_to_all.10.x_ref = bf16[64,16,256]{2,1,0:T(8,128)(2,1)S(1)} all-to-all(bf16[64,16,256]{2,1,0:T(8,128)(2,1)S(1)} %shard_map.73), channel_id=1, replica_groups=mesh['seq'=64,'tensor'=8] {'seq'}, dimensions={0} | all-to-all | bytes 1048576 | tf_op jit(solution)/shard_map/all_to_all | solution.py:203
  40.9 0.0 copy-start.2
  40.9 1.2 copy-done.2
  42.1 4.0 %shard_map.74 = bf16[64,16,128]{2,1,0:T(8,128)(2,1)S(1)} custom-call(bf16[64,16,256]{2,1,0:T(8,128)(2,1)S(1)} %all_to_all.10.x_ref, bf16[864,512]{1,0:T(8,128)(2,1)S(1)} %copy-done.2), custom_call_target="tpu_custom_call" | custom-call | tf_op jit(solution)/shard_map/pallas_call | solution.py:204
  46.1 18.0 %all_to_all.11.back_ref = bf16[64,16,128]{2,1,0:T(8,128)(2,1)S(1)} all-to-all(bf16[64,16,128]{2,1,0:T(8,128)(2,1)S(1)} %shard_map.74), channel_id=1, replica_groups=mesh['seq'=64,'tensor'=8] {'seq'}, dimensions={0} | all-to-all | bytes 524288 | tf_op jit(solution)/shard_map/all_to_all | solution.py:217
  64.0 0.0 copy-done.5
  64.0 0.0 copy-done.1
  64.0 0.0 copy-done.4
  64.0 0.2 shard_map.75.refs_0_
  64.2 3.5 %collective-permute-start = (bf16[256,512]{1,0:T(8,128)(2,1)S(1)}, bf16[256,512]{1,0:T(8,128)(2,1)S(1)}, u32[]{:S(2)}, u32[]{:S(2)}) collective-permute-start(bf16[256,512]{1,0:T(8,128)(2,1)S(1)} %shard_map.75.refs_0_), channel_id=1, source_target_pairs={{0,1},{1,2},{2,3},{3,4},{4,5},{5,6},{6,7},{7,0},{8,9},{9,10},{10,1... | collective-permute-start | bytes 786440 | tf_op jit(solution)/shard_map/ppermute | solution.py:228
  67.7 2.4 %collective-permute-start.1 = (bf16[256,512]{1,0:T(8,128)(2,1)S(1)}, bf16[256,512]{1,0:T(8,128)(2,1)S(1)}, u32[]{:S(2)}, u32[]{:S(2)}) collective-permute-start(bf16[256,512]{1,0:T(8,128)(2,1)S(1)} %shard_map.75.refs_0_), channel_id=1, source_target_pairs={{0,7},{1,0},{2,1},{3,2},{4,3},{5,4},{6,5},{7,6},{8,15},{9,8},{10,9... | collective-permute-start | bytes 786440 | tf_op jit(solution)/shard_map/ppermute | solution.py:229
  70.1 4.4 %collective-permute-done.refs_1_ = bf16[256,512]{1,0:T(8,128)(2,1)S(1)} collective-permute-done((bf16[256,512]{1,0:T(8,128)(2,1)S(1)}, bf16[256,512]{1,0:T(8,128)(2,1)S(1)}, u32[]{:S(2)}, u32[]{:S(2)}) %collective-permute-start) | collective-permute-done | bytes 262176 | tf_op jit(solution)/shard_map/ppermute | solution.py:228
  74.4 3.8 %collective-permute-start.2 = (bf16[256,512]{1,0:T(8,128)(2,1)S(1)}, bf16[256,512]{1,0:T(8,128)(2,1)S(1)}, u32[]{:S(2)}, u32[]{:S(2)}) collective-permute-start(bf16[256,512]{1,0:T(8,128)(2,1)S(1)} %collective-permute-done.refs_1_), channel_id=1, source_target_pairs={{0,1},{1,2},{2,3},{3,4},{4,5},{5,6},{6,7},{7,0},{8,9},{9,10},{10,1... | collective-permute-start | bytes 786440 | tf_op jit(solution)/shard_map/ppermute | solution.py:228
  78.2 0.5 collective-permute-done.1.refs_2_
  78.7 1.9 %collective-permute-start.3 = (bf16[256,512]{1,0:T(8,128)(2,1)S(1)}, bf16[256,512]{1,0:T(8,128)(2,1)S(1)}, u32[]{:S(2)}, u32[]{:S(2)}) collective-permute-start(bf16[256,512]{1,0:T(8,128)(2,1)S(1)} %collective-permute-done.1.refs_2_), channel_id=1, source_target_pairs={{0,7},{1,0},{2,1},{3,2},{4,3},{5,4},{6,5},{7,6},{8,15},{9,8},{10,9... | collective-permute-start | bytes 786440 | tf_op jit(solution)/shard_map/ppermute | solution.py:229
  80.6 3.3 %collective-permute-done.2.refs_3_ = bf16[256,512]{1,0:T(8,128)(2,1)S(1)} collective-permute-done((bf16[256,512]{1,0:T(8,128)(2,1)S(1)}, bf16[256,512]{1,0:T(8,128)(2,1)S(1)}, u32[]{:S(2)}, u32[]{:S(2)}) %collective-permute-start.2) | collective-permute-done | bytes 262176 | tf_op jit(solution)/shard_map/ppermute | solution.py:228
  83.9 5.0 %collective-permute-start.4 = (bf16[256,512]{1,0:T(8,128)(2,1)S(1)}, bf16[256,512]{1,0:T(8,128)(2,1)S(1)}, u32[]{:S(2)}, u32[]{:S(2)}) collective-permute-start(bf16[256,512]{1,0:T(8,128)(2,1)S(1)} %collective-permute-done.2.refs_3_), channel_id=1, source_target_pairs={{0,1},{1,2},{2,3},{3,4},{4,5},{5,6},{6,7},{7,0},{8,9},{9,10},{10,1... | collective-permute-start | bytes 786440 | tf_op jit(solution)/shard_map/ppermute | solution.py:232
  88.9 0.5 collective-permute-done.3.refs_4_
  89.4 1.9 %collective-permute-start.5 = (bf16[256,512]{1,0:T(8,128)(2,1)S(1)}, bf16[256,512]{1,0:T(8,128)(2,1)S(1)}, u32[]{:S(2)}, u32[]{:S(2)}) collective-permute-start(bf16[256,512]{1,0:T(8,128)(2,1)S(1)} %collective-permute-done.3.refs_4_), channel_id=1, source_target_pairs={{0,7},{1,0},{2,1},{3,2},{4,3},{5,4},{6,5},{7,6},{8,15},{9,8},{10,9... | collective-permute-start | bytes 786440 | tf_op jit(solution)/shard_map/ppermute | solution.py:233
  91.3 7.8 %collective-permute-start.6 = (bf16[128,512]{1,0:T(8,128)(2,1)S(1)}, bf16[128,512]{1,0:T(8,128)(2,1)S(1)}, u32[]{:S(2)}, u32[]{:S(2)}) collective-permute-start(bf16[128,512]{1,0:T(8,128)(2,1)S(1)} %slice.8), channel_id=1, source_target_pairs={{0,2},{1,3},{2,4},{3,5},{4,6},{5,7},{6,0},{7,1},{8,10},{9,11},{10,... | collective-permute-start | bytes 393224 | tf_op jit(solution)/shard_map/ppermute | solution.py:234
  99.2 1.9 %collective-permute-start.7 = (bf16[128,512]{1,0:T(8,128)(2,1)S(1)}, bf16[128,512]{1,0:T(8,128)(2,1)S(1)}, u32[]{:S(2)}, u32[]{:S(2)}) collective-permute-start(bf16[128,512]{1,0:T(8,128)(2,1)S(1)} %slice.9), channel_id=1, source_target_pairs={{0,6},{1,7},{2,0},{3,1},{4,2},{5,3},{6,4},{7,5},{8,14},{9,15},{10,... | collective-permute-start | bytes 393224 | tf_op jit(solution)/shard_map/ppermute | solution.py:235
  101.1 0.0 copy-done.6
  101.1 0.0 collective-permute-done.4.refs_5_
  101.1 0.0 collective-permute-done.5.refs_6_
  101.1 0.0 all-gather.2.cloned.1.call-done.refs_7_
  101.2 3.2 %shard_map.76 = (f32[256,512]{1,0:T(8,128)S(1)}, bf16[512,512]{1,0:T(8,128)(2,1)S(1)}) custom-call(s32[8]{0:T(128)S(1)} %and_select_fusion.index_ref, bf16[256,512]{1,0:T(8,128)(2,1)S(1)} %shard_map.75.refs_0_, bf16[256,512]{1,0:T(8,128)(2,1)S(1)} %collective-permute-done.refs_1_, bf16[256,512]{1,0:T(8,128)(2,1)S(1)} %collective-permute-done.1.refs_2_, ...), custom_call_target="tpu_custom_call" | custom-call | tf_op jit(solution)/shard_map/pallas_call | solution.py:241
  104.4 0.0 collective-permute-done.6.up_ref
  104.4 4.8 %collective-permute-done.7.down_ref = bf16[128,512]{1,0:T(8,128)(2,1)S(1)} collective-permute-done((bf16[128,512]{1,0:T(8,128)(2,1)S(1)}, bf16[128,512]{1,0:T(8,128)(2,1)S(1)}, u32[]{:S(2)}, u32[]{:S(2)}) %collective-permute-start.7) | collective-permute-done | bytes 131104 | tf_op jit(solution)/shard_map/ppermute | solution.py:235
  109.2 1.0 shard_map.77
  (3 shorter events, 0.0 us)
Async XLA Ops:
  6.5 94.5 %copy-start.6 = (s32[8]{0:T(128)S(1)}, s32[8]{0:T(128)}, u32[]{:S(2)}) copy-start(s32[8]{0:T(128)} %constant.24.clone) | copy-start | bytes 100
  6.5 57.5 %copy-start.5 = (f32[512]{0:T(512)S(1)}, f32[512]{0:T(512)}, u32[]{:S(2)}) copy-start(f32[512]{0:T(512)} %param.10) | copy-start | bytes 6148
  6.5 94.6 %all-gather.2.cloned.1.call-start = ((), (), s32[]{:S(2)}) async-start(), calls=%async_computation.2 | async-start | bytes 4259840 | tf_op jit(solution)/shard_map/all_gather | solution.py:192
  7.3 1.0 copy-start
  8.2 1.0 copy-start.3
  9.3 54.8 %copy-start.1 = (bf16[256,512]{1,0:T(8,128)(2,1)S(1)}, bf16[256,512]{1,0:T(8,128)(2,1)}, u32[]{:S(2)}) copy-start(bf16[256,512]{1,0:T(8,128)(2,1)} %signal_ref.3) | copy-start | bytes 786436
  9.3 54.8 %copy-start.4 = (bf16[256,512]{1,0:T(8,128)(2,1)S(1)}, bf16[256,512]{1,0:T(8,128)(2,1)}, u32[]{:S(2)}) copy-start(bf16[256,512]{1,0:T(8,128)(2,1)} %gating_ref.1) | copy-start | bytes 786436
  40.9 1.2 %copy-start.2 = (bf16[864,512]{1,0:T(8,128)(2,1)S(1)}, bf16[864,512]{1,0:T(8,128)(2,1)}, u32[]{:S(2)}) copy-start(bf16[864,512]{1,0:T(8,128)(2,1)} %constant.23.clone.table_ref) | copy-start | bytes 2654212
  64.2 10.2 %collective-permute-start = (bf16[256,512]{1,0:T(8,128)(2,1)S(1)}, bf16[256,512]{1,0:T(8,128)(2,1)S(1)}, u32[]{:S(2)}, u32[]{:S(2)}) collective-permute-start(bf16[256,512]{1,0:T(8,128)(2,1)S(1)} %shard_map.75.refs_0_), channel_id=1, source_target_pairs={{0,1},{1,2},{2,3},{3,4},{4,5},{5,6},{6,7},{7,0},{8,9},{9,10},{10,1... | collective-permute-start | bytes 786440 | tf_op jit(solution)/shard_map/ppermute | solution.py:228
  67.7 11.0 %collective-permute-start.1 = (bf16[256,512]{1,0:T(8,128)(2,1)S(1)}, bf16[256,512]{1,0:T(8,128)(2,1)S(1)}, u32[]{:S(2)}, u32[]{:S(2)}) collective-permute-start(bf16[256,512]{1,0:T(8,128)(2,1)S(1)} %shard_map.75.refs_0_), channel_id=1, source_target_pairs={{0,7},{1,0},{2,1},{3,2},{4,3},{5,4},{6,5},{7,6},{8,15},{9,8},{10,9... | collective-permute-start | bytes 786440 | tf_op jit(solution)/shard_map/ppermute | solution.py:229
  74.4 9.5 %collective-permute-start.2 = (bf16[256,512]{1,0:T(8,128)(2,1)S(1)}, bf16[256,512]{1,0:T(8,128)(2,1)S(1)}, u32[]{:S(2)}, u32[]{:S(2)}) collective-permute-start(bf16[256,512]{1,0:T(8,128)(2,1)S(1)} %collective-permute-done.refs_1_), channel_id=1, source_target_pairs={{0,1},{1,2},{2,3},{3,4},{4,5},{5,6},{6,7},{7,0},{8,9},{9,10},{10,1... | collective-permute-start | bytes 786440 | tf_op jit(solution)/shard_map/ppermute | solution.py:228
  78.7 10.7 %collective-permute-start.3 = (bf16[256,512]{1,0:T(8,128)(2,1)S(1)}, bf16[256,512]{1,0:T(8,128)(2,1)S(1)}, u32[]{:S(2)}, u32[]{:S(2)}) collective-permute-start(bf16[256,512]{1,0:T(8,128)(2,1)S(1)} %collective-permute-done.1.refs_2_), channel_id=1, source_target_pairs={{0,7},{1,0},{2,1},{3,2},{4,3},{5,4},{6,5},{7,6},{8,15},{9,8},{10,9... | collective-permute-start | bytes 786440 | tf_op jit(solution)/shard_map/ppermute | solution.py:229
  83.9 17.2 %collective-permute-start.4 = (bf16[256,512]{1,0:T(8,128)(2,1)S(1)}, bf16[256,512]{1,0:T(8,128)(2,1)S(1)}, u32[]{:S(2)}, u32[]{:S(2)}) collective-permute-start(bf16[256,512]{1,0:T(8,128)(2,1)S(1)} %collective-permute-done.2.refs_3_), channel_id=1, source_target_pairs={{0,1},{1,2},{2,3},{3,4},{4,5},{5,6},{6,7},{7,0},{8,9},{9,10},{10,1... | collective-permute-start | bytes 786440 | tf_op jit(solution)/shard_map/ppermute | solution.py:232
  89.4 11.7 %collective-permute-start.5 = (bf16[256,512]{1,0:T(8,128)(2,1)S(1)}, bf16[256,512]{1,0:T(8,128)(2,1)S(1)}, u32[]{:S(2)}, u32[]{:S(2)}) collective-permute-start(bf16[256,512]{1,0:T(8,128)(2,1)S(1)} %collective-permute-done.3.refs_4_), channel_id=1, source_target_pairs={{0,7},{1,0},{2,1},{3,2},{4,3},{5,4},{6,5},{7,6},{8,15},{9,8},{10,9... | collective-permute-start | bytes 786440 | tf_op jit(solution)/shard_map/ppermute | solution.py:233
  91.3 13.0 %collective-permute-start.6 = (bf16[128,512]{1,0:T(8,128)(2,1)S(1)}, bf16[128,512]{1,0:T(8,128)(2,1)S(1)}, u32[]{:S(2)}, u32[]{:S(2)}) collective-permute-start(bf16[128,512]{1,0:T(8,128)(2,1)S(1)} %slice.8), channel_id=1, source_target_pairs={{0,2},{1,3},{2,4},{3,5},{4,6},{5,7},{6,0},{7,1},{8,10},{9,11},{10,... | collective-permute-start | bytes 393224 | tf_op jit(solution)/shard_map/ppermute | solution.py:234
  99.2 10.0 %collective-permute-start.7 = (bf16[128,512]{1,0:T(8,128)(2,1)S(1)}, bf16[128,512]{1,0:T(8,128)(2,1)S(1)}, u32[]{:S(2)}, u32[]{:S(2)}) collective-permute-start(bf16[128,512]{1,0:T(8,128)(2,1)S(1)} %slice.9), channel_id=1, source_target_pairs={{0,6},{1,7},{2,0},{3,1},{4,2},{5,3},{6,4},{7,5},{8,14},{9,15},{10,... | collective-permute-start | bytes 393224 | tf_op jit(solution)/shard_map/ppermute | solution.py:235
Sparse Core Ops, SparseCore 0:
  10.7 90.1 all-gather.1

commit v6 on v3

--- a/solution.py
+++ b/solution.py
@@ -83,6 +83,13 @@
         mid[(2 * n + 1) * inner : (2 * n + 2) * inner, inner:] = cos
 
 
+def three_products(cat, mid, rows):
+    depth = mid.shape[0] // 2
+    product = jnp.dot(cat[:rows, :depth], mid[:depth, :], preferred_element_type=F32)
+    product += jnp.dot(cat[:rows, :depth], mid[depth:, :], preferred_element_type=F32)
+    return product + jnp.dot(cat[:rows, depth:], mid[:depth, :], preferred_element_type=F32)
+
+
 def conv_kernel(places, x_ref, table_ref, out_ref, flat, cat, spec, back, mid, turn):
     parts = [table_ref.at[pl.ds(start, end - start), pl.ds(0, width)] for start, end, width in places]
     short_ref, turn_ref, first_ref, last_ref = parts
@@ -112,11 +119,11 @@
                     [real * cos_ref[...] + imag * sin_ref[...], imag * cos_ref[...] - real * sin_ref[...]], axis=1
                 )
             )
-        both = jnp.concatenate(parts, axis=0).astype(BF16)
+        high, low = split(jnp.concatenate(parts, axis=0))
         here = pl.ds(c * 2 * held, 2 * held)
-        cat[here, : 2 * inner] = both
-        cat[here, 2 * inner :] = both
-    spec[...] = jnp.dot(cat[...], mid[...], preferred_element_type=F32)
+        cat[here, : 2 * inner] = high
+        cat[here, 2 * inner :] = low
+    spec[...] = three_products(cat, mid, chans * 2 * held)
     for c in range(0, chans, 2):
         parts = []
         for one in (c, c + 1):
@@ -124,12 +131,12 @@
             k = spec[pl.ds(one * 2 * held + held, held), :]
             sr, si, kr, ki = s[:, :inner], s[:, inner:], k[:, :inner], k[:, inner:]
             parts.append(jnp.concatenate([sr * kr - si * ki, -(sr * ki + si * kr)], axis=1))
-        both = jnp.concatenate(parts, axis=0).astype(BF16)
+        high, low = split(jnp.concatenate(parts, axis=0))
         here = pl.ds(c * held, 2 * held)
-        cat[here, : 2 * inner] = both
-        cat[here, 2 * inner :] = both
+        cat[here, : 2 * inner] = high
+        cat[here, 2 * inner :] = low
     half = chans * held
-    spec[:half, :] = jnp.dot(cat[:half, :], mid[...], preferred_element_type=F32)
+    spec[:half, :] = three_products(cat, mid, half)
     for c in range(chans):
         q = spec[pl.ds(c * held, held), :]
         qr, qi = q[:, :inner], -q[:, inner:]

time: 117 us -> 117 us (level)
  the two profiles are of different devices: /device:TPU:30 before, /device:TPU:24 now
where the time goes in v6:
time: 117 us
  blocking collectives  49.4 us (42%)
  starting transfers between devices  29.2 us (25%)
  between operations  13.6 us (12%)
  waiting for transfers between devices  12.9 us (11%)
  Pallas kernels  8.52 us (7%)
  local copies, waits for them, and re-layouts  3.19 us (3%)
    all_to_all x1, blocking collectives, body(): lax.all_to_all(packed, 'seq', split_axis=0, concat_axis=0, tiled=True)  31.3 us
    all_to_all x1, blocking collectives, body(): lax.all_to_all(convolved, 'seq', split_axis=0, concat_axis=0, tiled=True)  18.1 us
    ppermute x3, starting transfers between devices, body(): up = lax.ppermute(up, 'tensor', up_pairs)  15.9 us
    ppermute x3, waiting for transfers between devices, body(): up = lax.ppermute(up, 'tensor', up_pairs)  9.26 us
    ppermute x3, starting transfers between devices, body(): down = lax.ppermute(down, 'tensor', down_pairs)  5.76 us
    ppermute x1, starting transfers between devices, body(): up = lax.ppermute(up[:tokens // 2], 'tensor', up_pairs)  5.6 us
    pallas_call x1, Pallas kernels, body(): pl.pallas_call(functools.partial(conv_kernel, places), out_shape=jax.Shap...  3.96 us
    pallas_call x1, Pallas kernels, body(): pl.pallas_call(project_kernel, in_specs=[pl.BlockSpec(memory_space=pltpu....  3.19 us
  transfers between devices with their start and end apart: 9, of which 4 were waited for; matrix products, arithmetic and copies ran while one was open for 0% of the time, Pallas kernels for 6%

profile of v6, /device:TPU:24, one launch (start us, length us, event | category | flops | bytes accessed | tf_op | source)
XLA Modules:
  0.0 116.8 jit_solution(6715562157363366806)
XLA Ops:
  6.5 0.0 copy-start.6
  6.5 0.0 copy-start.5
  6.5 0.0 all-gather.2.cloned.1.call-start
  6.5 0.7 all-gather.2.cloned.1.call-update
  7.3 0.0 copy-start
  7.3 0.9 copy-done
  8.2 0.0 copy-start.3
  8.2 1.0 copy-done.3
  9.3 0.0 copy-start.1
  9.3 0.0 copy-start.4
  9.3 0.2 shard_map.73
  9.5 31.3 %all_to_all.10.x_ref = bf16[64,16,256]{2,1,0:T(8,128)(2,1)S(1)} all-to-all(bf16[64,16,256]{2,1,0:T(8,128)(2,1)S(1)} %shard_map.73), channel_id=1, replica_groups=mesh['seq'=64,'tensor'=8] {'seq'}, dimensions={0} | all-to-all | bytes 1048576 | tf_op jit(solution)/shard_map/all_to_all | solution.py:208
  40.8 0.0 copy-start.2
  40.8 1.2 %copy-done.2 = bf16[864,512]{1,0:T(8,128)(2,1)S(1)} copy-done((bf16[864,512]{1,0:T(8,128)(2,1)S(1)}, bf16[864,512]{1,0:T(8,128)(2,1)}, u32[]{:S(2)}) %copy-start.2) | copy-done | bytes 884760
  42.0 4.0 %shard_map.74 = bf16[64,16,128]{2,1,0:T(8,128)(2,1)S(1)} custom-call(bf16[64,16,256]{2,1,0:T(8,128)(2,1)S(1)} %all_to_all.10.x_ref, bf16[864,512]{1,0:T(8,128)(2,1)S(1)} %copy-done.2), custom_call_target="tpu_custom_call" | custom-call | tf_op jit(solution)/shard_map/pallas_call | solution.py:209
  45.9 18.1 %all_to_all.11.back_ref = bf16[64,16,128]{2,1,0:T(8,128)(2,1)S(1)} all-to-all(bf16[64,16,128]{2,1,0:T(8,128)(2,1)S(1)} %shard_map.74), channel_id=1, replica_groups=mesh['seq'=64,'tensor'=8] {'seq'}, dimensions={0} | all-to-all | bytes 524288 | tf_op jit(solution)/shard_map/all_to_all | solution.py:222
  64.0 0.0 copy-done.5
  64.0 0.0 copy-done.1
  64.0 0.0 copy-done.4
  64.0 0.2 shard_map.75.refs_0_
  64.2 4.7 %collective-permute-start = (bf16[256,512]{1,0:T(8,128)(2,1)S(1)}, bf16[256,512]{1,0:T(8,128)(2,1)S(1)}, u32[]{:S(2)}, u32[]{:S(2)}) collective-permute-start(bf16[256,512]{1,0:T(8,128)(2,1)S(1)} %shard_map.75.refs_0_), channel_id=1, source_target_pairs={{0,1},{1,2},{2,3},{3,4},{4,5},{5,6},{6,7},{7,0},{8,9},{9,10},{10,1... | collective-permute-start | bytes 786440 | tf_op jit(solution)/shard_map/ppermute | solution.py:231
  68.9 1.9 %collective-permute-start.1 = (bf16[256,512]{1,0:T(8,128)(2,1)S(1)}, bf16[256,512]{1,0:T(8,128)(2,1)S(1)}, u32[]{:S(2)}, u32[]{:S(2)}) collective-permute-start(bf16[256,512]{1,0:T(8,128)(2,1)S(1)} %shard_map.75.refs_0_), channel_id=1, source_target_pairs={{0,7},{1,0},{2,1},{3,2},{4,3},{5,4},{6,5},{7,6},{8,15},{9,8},{10,9... | collective-permute-start | bytes 786440 | tf_op jit(solution)/shard_map/ppermute | solution.py:232
  70.8 3.9 %collective-permute-done.refs_1_ = bf16[256,512]{1,0:T(8,128)(2,1)S(1)} collective-permute-done((bf16[256,512]{1,0:T(8,128)(2,1)S(1)}, bf16[256,512]{1,0:T(8,128)(2,1)S(1)}, u32[]{:S(2)}, u32[]{:S(2)}) %collective-permute-start) | collective-permute-done | bytes 262176 | tf_op jit(solution)/shard_map/ppermute | solution.py:231
  74.7 5.6 %collective-permute-start.2 = (bf16[256,512]{1,0:T(8,128)(2,1)S(1)}, bf16[256,512]{1,0:T(8,128)(2,1)S(1)}, u32[]{:S(2)}, u32[]{:S(2)}) collective-permute-start(bf16[256,512]{1,0:T(8,128)(2,1)S(1)} %collective-permute-done.refs_1_), channel_id=1, source_target_pairs={{0,1},{1,2},{2,3},{3,4},{4,5},{5,6},{6,7},{7,0},{8,9},{9,10},{10,1... | collective-permute-start | bytes 786440 | tf_op jit(solution)/shard_map/ppermute | solution.py:231
  80.3 0.0 collective-permute-done.1.refs_2_
  80.3 1.9 %collective-permute-start.3 = (bf16[256,512]{1,0:T(8,128)(2,1)S(1)}, bf16[256,512]{1,0:T(8,128)(2,1)S(1)}, u32[]{:S(2)}, u32[]{:S(2)}) collective-permute-start(bf16[256,512]{1,0:T(8,128)(2,1)S(1)} %collective-permute-done.1.refs_2_), channel_id=1, source_target_pairs={{0,7},{1,0},{2,1},{3,2},{4,3},{5,4},{6,5},{7,6},{8,15},{9,8},{10,9... | collective-permute-start | bytes 786440 | tf_op jit(solution)/shard_map/ppermute | solution.py:232
  82.3 3.1 %collective-permute-done.2.refs_3_ = bf16[256,512]{1,0:T(8,128)(2,1)S(1)} collective-permute-done((bf16[256,512]{1,0:T(8,128)(2,1)S(1)}, bf16[256,512]{1,0:T(8,128)(2,1)S(1)}, u32[]{:S(2)}, u32[]{:S(2)}) %collective-permute-start.2) | collective-permute-done | bytes 262176 | tf_op jit(solution)/shard_map/ppermute | solution.py:231
  85.4 5.6 %collective-permute-start.4 = (bf16[256,512]{1,0:T(8,128)(2,1)S(1)}, bf16[256,512]{1,0:T(8,128)(2,1)S(1)}, u32[]{:S(2)}, u32[]{:S(2)}) collective-permute-start(bf16[256,512]{1,0:T(8,128)(2,1)S(1)} %collective-permute-done.2.refs_3_), channel_id=1, source_target_pairs={{0,1},{1,2},{2,3},{3,4},{4,5},{5,6},{6,7},{7,0},{8,9},{9,10},{10,1... | collective-permute-start | bytes 786440 | tf_op jit(solution)/shard_map/ppermute | solution.py:231
  91.0 0.0 collective-permute-done.3.refs_4_
  91.0 1.9 %collective-permute-start.5 = (bf16[256,512]{1,0:T(8,128)(2,1)S(1)}, bf16[256,512]{1,0:T(8,128)(2,1)S(1)}, u32[]{:S(2)}, u32[]{:S(2)}) collective-permute-start(bf16[256,512]{1,0:T(8,128)(2,1)S(1)} %collective-permute-done.3.refs_4_), channel_id=1, source_target_pairs={{0,7},{1,0},{2,1},{3,2},{4,3},{5,4},{6,5},{7,6},{8,15},{9,8},{10,9... | collective-permute-start | bytes 786440 | tf_op jit(solution)/shard_map/ppermute | solution.py:232
  93.0 2.2 %collective-permute-done.4.refs_5_ = bf16[256,512]{1,0:T(8,128)(2,1)S(1)} collective-permute-done((bf16[256,512]{1,0:T(8,128)(2,1)S(1)}, bf16[256,512]{1,0:T(8,128)(2,1)S(1)}, u32[]{:S(2)}, u32[]{:S(2)}) %collective-permute-start.4) | collective-permute-done | bytes 262176 | tf_op jit(solution)/shard_map/ppermute | solution.py:231
  95.2 5.6 %collective-permute-start.6 = (bf16[128,512]{1,0:T(8,128)(2,1)S(1)}, bf16[128,512]{1,0:T(8,128)(2,1)S(1)}, u32[]{:S(2)}, u32[]{:S(2)}) collective-permute-start(bf16[128,512]{1,0:T(8,128)(2,1)S(1)} %slice.8), channel_id=1, source_target_pairs={{0,1},{1,2},{2,3},{3,4},{4,5},{5,6},{6,7},{7,0},{8,9},{9,10},{10,1... | collective-permute-start | bytes 393224 | tf_op jit(solution)/shard_map/ppermute | solution.py:235
  100.8 0.0 collective-permute-done.5.refs_6_
  100.8 1.9 %collective-permute-start.7 = (bf16[128,512]{1,0:T(8,128)(2,1)S(1)}, bf16[128,512]{1,0:T(8,128)(2,1)S(1)}, u32[]{:S(2)}, u32[]{:S(2)}) collective-permute-start(bf16[128,512]{1,0:T(8,128)(2,1)S(1)} %slice.9), channel_id=1, source_target_pairs={{0,7},{1,0},{2,1},{3,2},{4,3},{5,4},{6,5},{7,6},{8,15},{9,8},{10,9... | collective-permute-start | bytes 393224 | tf_op jit(solution)/shard_map/ppermute | solution.py:236
  102.8 0.0 copy-done.6
  102.8 0.0 all-gather.2.cloned.1.call-done.refs_7_
  102.8 3.2 %shard_map.76 = (f32[256,512]{1,0:T(8,128)S(1)}, bf16[512,512]{1,0:T(8,128)(2,1)S(1)}) custom-call(s32[8]{0:T(128)S(1)} %and_select_fusion.index_ref, bf16[256,512]{1,0:T(8,128)(2,1)S(1)} %shard_map.75.refs_0_, bf16[256,512]{1,0:T(8,128)(2,1)S(1)} %collective-permute-done.refs_1_, bf16[256,512]{1,0:T(8,128)(2,1)S(1)} %collective-permute-done.1.refs_2_, ...), custom_call_target="tpu_custom_call" | custom-call | tf_op jit(solution)/shard_map/pallas_call | solution.py:239
  106.0 0.0 collective-permute-done.6.up_ref
  106.0 2.9 %collective-permute-done.7.down_ref = bf16[128,512]{1,0:T(8,128)(2,1)S(1)} collective-permute-done((bf16[128,512]{1,0:T(8,128)(2,1)S(1)}, bf16[128,512]{1,0:T(8,128)(2,1)S(1)}, u32[]{:S(2)}, u32[]{:S(2)}) %collective-permute-start.7) | collective-permute-done | bytes 131104 | tf_op jit(solution)/shard_map/ppermute | solution.py:236
  108.9 1.0 shard_map.77
  (3 shorter events, 0.0 us)
Async XLA Ops:
  6.5 96.2 %copy-start.6 = (s32[8]{0:T(128)S(1)}, s32[8]{0:T(128)}, u32[]{:S(2)}) copy-start(s32[8]{0:T(128)} %constant.24.clone) | copy-start | bytes 100
  6.5 57.5 %copy-start.5 = (f32[512]{0:T(512)S(1)}, f32[512]{0:T(512)}, u32[]{:S(2)}) copy-start(f32[512]{0:T(512)} %param.10) | copy-start | bytes 6148
  6.5 96.3 %all-gather.2.cloned.1.call-start = ((), (), s32[]{:S(2)}) async-start(), calls=%async_computation.2 | async-start | bytes 4259840 | tf_op jit(solution)/shard_map/all_gather | solution.py:197
  7.3 1.0 copy-start
  8.2 1.0 copy-start.3
  9.3 54.7 %copy-start.1 = (bf16[256,512]{1,0:T(8,128)(2,1)S(1)}, bf16[256,512]{1,0:T(8,128)(2,1)}, u32[]{:S(2)}) copy-start(bf16[256,512]{1,0:T(8,128)(2,1)} %signal_ref.3) | copy-start | bytes 786436
  9.3 54.7 %copy-start.4 = (bf16[256,512]{1,0:T(8,128)(2,1)S(1)}, bf16[256,512]{1,0:T(8,128)(2,1)}, u32[]{:S(2)}) copy-start(bf16[256,512]{1,0:T(8,128)(2,1)} %gating_ref.1) | copy-start | bytes 786436
  40.8 1.2 %copy-start.2 = (bf16[864,512]{1,0:T(8,128)(2,1)S(1)}, bf16[864,512]{1,0:T(8,128)(2,1)}, u32[]{:S(2)}) copy-start(bf16[864,512]{1,0:T(8,128)(2,1)} %constant.23.clone.table_ref) | copy-start | bytes 2654212
  64.2 10.6 %collective-permute-start = (bf16[256,512]{1,0:T(8,128)(2,1)S(1)}, bf16[256,512]{1,0:T(8,128)(2,1)S(1)}, u32[]{:S(2)}, u32[]{:S(2)}) collective-permute-start(bf16[256,512]{1,0:T(8,128)(2,1)S(1)} %shard_map.75.refs_0_), channel_id=1, source_target_pairs={{0,1},{1,2},{2,3},{3,4},{4,5},{5,6},{6,7},{7,0},{8,9},{9,10},{10,1... | collective-permute-start | bytes 786440 | tf_op jit(solution)/shard_map/ppermute | solution.py:231
  68.9 11.4 %collective-permute-start.1 = (bf16[256,512]{1,0:T(8,128)(2,1)S(1)}, bf16[256,512]{1,0:T(8,128)(2,1)S(1)}, u32[]{:S(2)}, u32[]{:S(2)}) collective-permute-start(bf16[256,512]{1,0:T(8,128)(2,1)S(1)} %shard_map.75.refs_0_), channel_id=1, source_target_pairs={{0,7},{1,0},{2,1},{3,2},{4,3},{5,4},{6,5},{7,6},{8,15},{9,8},{10,9... | collective-permute-start | bytes 786440 | tf_op jit(solution)/shard_map/ppermute | solution.py:232
  74.7 10.7 %collective-permute-start.2 = (bf16[256,512]{1,0:T(8,128)(2,1)S(1)}, bf16[256,512]{1,0:T(8,128)(2,1)S(1)}, u32[]{:S(2)}, u32[]{:S(2)}) collective-permute-start(bf16[256,512]{1,0:T(8,128)(2,1)S(1)} %collective-permute-done.refs_1_), channel_id=1, source_target_pairs={{0,1},{1,2},{2,3},{3,4},{4,5},{5,6},{6,7},{7,0},{8,9},{9,10},{10,1... | collective-permute-start | bytes 786440 | tf_op jit(solution)/shard_map/ppermute | solution.py:231
  80.3 10.7 %collective-permute-start.3 = (bf16[256,512]{1,0:T(8,128)(2,1)S(1)}, bf16[256,512]{1,0:T(8,128)(2,1)S(1)}, u32[]{:S(2)}, u32[]{:S(2)}) collective-permute-start(bf16[256,512]{1,0:T(8,128)(2,1)S(1)} %collective-permute-done.1.refs_2_), channel_id=1, source_target_pairs={{0,7},{1,0},{2,1},{3,2},{4,3},{5,4},{6,5},{7,6},{8,15},{9,8},{10,9... | collective-permute-start | bytes 786440 | tf_op jit(solution)/shard_map/ppermute | solution.py:232
  85.4 9.8 %collective-permute-start.4 = (bf16[256,512]{1,0:T(8,128)(2,1)S(1)}, bf16[256,512]{1,0:T(8,128)(2,1)S(1)}, u32[]{:S(2)}, u32[]{:S(2)}) collective-permute-start(bf16[256,512]{1,0:T(8,128)(2,1)S(1)} %collective-permute-done.2.refs_3_), channel_id=1, source_target_pairs={{0,1},{1,2},{2,3},{3,4},{4,5},{5,6},{6,7},{7,0},{8,9},{9,10},{10,1... | collective-permute-start | bytes 786440 | tf_op jit(solution)/shard_map/ppermute | solution.py:231
  91.0 9.8 %collective-permute-start.5 = (bf16[256,512]{1,0:T(8,128)(2,1)S(1)}, bf16[256,512]{1,0:T(8,128)(2,1)S(1)}, u32[]{:S(2)}, u32[]{:S(2)}) collective-permute-start(bf16[256,512]{1,0:T(8,128)(2,1)S(1)} %collective-permute-done.3.refs_4_), channel_id=1, source_target_pairs={{0,7},{1,0},{2,1},{3,2},{4,3},{5,4},{6,5},{7,6},{8,15},{9,8},{10,9... | collective-permute-start | bytes 786440 | tf_op jit(solution)/shard_map/ppermute | solution.py:232
  95.2 10.8 %collective-permute-start.6 = (bf16[128,512]{1,0:T(8,128)(2,1)S(1)}, bf16[128,512]{1,0:T(8,128)(2,1)S(1)}, u32[]{:S(2)}, u32[]{:S(2)}) collective-permute-start(bf16[128,512]{1,0:T(8,128)(2,1)S(1)} %slice.8), channel_id=1, source_target_pairs={{0,1},{1,2},{2,3},{3,4},{4,5},{5,6},{6,7},{7,0},{8,9},{9,10},{10,1... | collective-permute-start | bytes 393224 | tf_op jit(solution)/shard_map/ppermute | solution.py:235
  100.8 8.1 %collective-permute-start.7 = (bf16[128,512]{1,0:T(8,128)(2,1)S(1)}, bf16[128,512]{1,0:T(8,128)(2,1)S(1)}, u32[]{:S(2)}, u32[]{:S(2)}) collective-permute-start(bf16[128,512]{1,0:T(8,128)(2,1)S(1)} %slice.9), channel_id=1, source_target_pairs={{0,7},{1,0},{2,1},{3,2},{4,3},{5,4},{6,5},{7,6},{8,15},{9,8},{10,9... | collective-permute-start | bytes 393224 | tf_op jit(solution)/shard_map/ppermute | solution.py:236
Sparse Core Ops, SparseCore 0:
  10.7 90.0 all-gather.1

commit v7 on v6

--- a/solution.py
+++ b/solution.py
@@ -107,18 +107,16 @@
             x_ref[:, :, h * lanes : (h + 1) * lanes].astype(F32).reshape(span, lanes)
         )
     for c in range(chans):
+        columns = [
+            flat[pl.ds(h * span + row, blocks, stride=rows), :] for row in (c, chans + c) for h in range(halves)
+        ]
+        x = jnp.concatenate(columns, axis=1).astype(BF16)
+        both = jnp.dot(first_ref[...], jnp.concatenate([x, x], axis=0), preferred_element_type=F32)
         parts = []
-        for row in (c, chans + c):
-            x = jnp.concatenate(
-                [flat[pl.ds(h * span + row, blocks, stride=rows), :] for h in range(halves)], axis=1
-            ).astype(BF16)
-            a = jnp.dot(first_ref[...], jnp.concatenate([x, x], axis=0), preferred_element_type=F32)
+        for a in (both[:, :inner], both[:, inner:]):
             real, imag = a[:held], a[held:]
-            parts.append(
-                jnp.concatenate(
-                    [real * cos_ref[...] + imag * sin_ref[...], imag * cos_ref[...] - real * sin_ref[...]], axis=1
-                )
-            )
+            turned = [real * cos_ref[...] + imag * sin_ref[...], imag * cos_ref[...] - real * sin_ref[...]]
+            parts.append(jnp.concatenate(turned, axis=1))
         high, low = split(jnp.concatenate(parts, axis=0))
         here = pl.ds(c * 2 * held, 2 * held)
         cat[here, : 2 * inner] = high

time: 117 us -> 117 us (level)
  no operation moved by 1% of the time
where the time goes in v7:
time: 117 us
  blocking collectives  49.4 us (42%)
  starting transfers between devices  29.2 us (25%)
  between operations  13.6 us (12%)
  waiting for transfers between devices  12.9 us (11%)
  Pallas kernels  8.52 us (7%)
  local copies, waits for them, and re-layouts  3.19 us (3%)
    all_to_all x1, blocking collectives, body(): lax.all_to_all(packed, 'seq', split_axis=0, concat_axis=0, tiled=True)  31.3 us
    all_to_all x1, blocking collectives, body(): lax.all_to_all(convolved, 'seq', split_axis=0, concat_axis=0, tiled=True)  18.1 us
    ppermute x3, starting transfers between devices, body(): up = lax.ppermute(up, 'tensor', up_pairs)  15.9 us
    ppermute x3, waiting for transfers between devices, body(): up = lax.ppermute(up, 'tensor', up_pairs)  9.26 us
    ppermute x3, starting transfers between devices, body(): down = lax.ppermute(down, 'tensor', down_pairs)  5.76 us
    ppermute x1, starting transfers between devices, body(): up = lax.ppermute(up[:tokens // 2], 'tensor', up_pairs)  5.6 us
    pallas_call x1, Pallas kernels, body(): pl.pallas_call(functools.partial(conv_kernel, places), out_shape=jax.Shap...  3.96 us
    pallas_call x1, Pallas kernels, body(): pl.pallas_call(project_kernel, in_specs=[pl.BlockSpec(memory_space=pltpu....  3.19 us
  transfers between devices with their start and end apart: 9, of which 4 were waited for; matrix products, arithmetic and copies ran while one was open for 0% of the time, Pallas kernels for 6%

profile of v7, /device:TPU:24, one launch (start us, length us, event | category | flops | bytes accessed | tf_op | source)
XLA Modules:
  0.0 116.8 jit_solution(6715562157363366806)
XLA Ops:
  6.5 0.0 copy-start.6
  6.5 0.0 copy-start.5
  6.5 0.0 all-gather.2.cloned.1.call-start
  6.5 0.7 all-gather.2.cloned.1.call-update
  7.3 0.0 copy-start
  7.3 0.9 copy-done
  8.2 0.0 copy-start.3
  8.2 1.0 copy-done.3
  9.3 0.0 copy-start.1
  9.3 0.0 copy-start.4
  9.3 0.2 shard_map.73
  9.5 31.3 %all_to_all.10.x_ref = bf16[64,16,256]{2,1,0:T(8,128)(2,1)S(1)} all-to-all(bf16[64,16,256]{2,1,0:T(8,128)(2,1)S(1)} %shard_map.73), channel_id=1, replica_groups=mesh['seq'=64,'tensor'=8] {'seq'}, dimensions={0} | all-to-all | bytes 1048576 | tf_op jit(solution)/shard_map/all_to_all | solution.py:206
  40.8 0.0 copy-start.2
  40.8 1.2 %copy-done.2 = bf16[864,512]{1,0:T(8,128)(2,1)S(1)} copy-done((bf16[864,512]{1,0:T(8,128)(2,1)S(1)}, bf16[864,512]{1,0:T(8,128)(2,1)}, u32[]{:S(2)}) %copy-start.2) | copy-done | bytes 884760
  42.0 4.0 %shard_map.74 = bf16[64,16,128]{2,1,0:T(8,128)(2,1)S(1)} custom-call(bf16[64,16,256]{2,1,0:T(8,128)(2,1)S(1)} %all_to_all.10.x_ref, bf16[864,512]{1,0:T(8,128)(2,1)S(1)} %copy-done.2), custom_call_target="tpu_custom_call" | custom-call | tf_op jit(solution)/shard_map/pallas_call | solution.py:207
  45.9 18.1 %all_to_all.11.back_ref = bf16[64,16,128]{2,1,0:T(8,128)(2,1)S(1)} all-to-all(bf16[64,16,128]{2,1,0:T(8,128)(2,1)S(1)} %shard_map.74), channel_id=1, replica_groups=mesh['seq'=64,'tensor'=8] {'seq'}, dimensions={0} | all-to-all | bytes 524288 | tf_op jit(solution)/shard_map/all_to_all | solution.py:220
  64.0 0.0 copy-done.5
  64.0 0.0 copy-done.1
  64.0 0.0 copy-done.4
  64.0 0.2 shard_map.75.refs_0_
  64.2 4.7 %collective-permute-start = (bf16[256,512]{1,0:T(8,128)(2,1)S(1)}, bf16[256,512]{1,0:T(8,128)(2,1)S(1)}, u32[]{:S(2)}, u32[]{:S(2)}) collective-permute-start(bf16[256,512]{1,0:T(8,128)(2,1)S(1)} %shard_map.75.refs_0_), channel_id=1, source_target_pairs={{0,1},{1,2},{2,3},{3,4},{4,5},{5,6},{6,7},{7,0},{8,9},{9,10},{10,1... | collective-permute-start | bytes 786440 | tf_op jit(solution)/shard_map/ppermute | solution.py:229
  68.9 1.9 %collective-permute-start.1 = (bf16[256,512]{1,0:T(8,128)(2,1)S(1)}, bf16[256,512]{1,0:T(8,128)(2,1)S(1)}, u32[]{:S(2)}, u32[]{:S(2)}) collective-permute-start(bf16[256,512]{1,0:T(8,128)(2,1)S(1)} %shard_map.75.refs_0_), channel_id=1, source_target_pairs={{0,7},{1,0},{2,1},{3,2},{4,3},{5,4},{6,5},{7,6},{8,15},{9,8},{10,9... | collective-permute-start | bytes 786440 | tf_op jit(solution)/shard_map/ppermute | solution.py:230
  70.8 3.9 %collective-permute-done.refs_1_ = bf16[256,512]{1,0:T(8,128)(2,1)S(1)} collective-permute-done((bf16[256,512]{1,0:T(8,128)(2,1)S(1)}, bf16[256,512]{1,0:T(8,128)(2,1)S(1)}, u32[]{:S(2)}, u32[]{:S(2)}) %collective-permute-start) | collective-permute-done | bytes 262176 | tf_op jit(solution)/shard_map/ppermute | solution.py:229
  74.7 5.6 %collective-permute-start.2 = (bf16[256,512]{1,0:T(8,128)(2,1)S(1)}, bf16[256,512]{1,0:T(8,128)(2,1)S(1)}, u32[]{:S(2)}, u32[]{:S(2)}) collective-permute-start(bf16[256,512]{1,0:T(8,128)(2,1)S(1)} %collective-permute-done.refs_1_), channel_id=1, source_target_pairs={{0,1},{1,2},{2,3},{3,4},{4,5},{5,6},{6,7},{7,0},{8,9},{9,10},{10,1... | collective-permute-start | bytes 786440 | tf_op jit(solution)/shard_map/ppermute | solution.py:229
  80.3 0.0 collective-permute-done.1.refs_2_
  80.3 1.9 %collective-permute-start.3 = (bf16[256,512]{1,0:T(8,128)(2,1)S(1)}, bf16[256,512]{1,0:T(8,128)(2,1)S(1)}, u32[]{:S(2)}, u32[]{:S(2)}) collective-permute-start(bf16[256,512]{1,0:T(8,128)(2,1)S(1)} %collective-permute-done.1.refs_2_), channel_id=1, source_target_pairs={{0,7},{1,0},{2,1},{3,2},{4,3},{5,4},{6,5},{7,6},{8,15},{9,8},{10,9... | collective-permute-start | bytes 786440 | tf_op jit(solution)/shard_map/ppermute | solution.py:230
  82.3 3.1 %collective-permute-done.2.refs_3_ = bf16[256,512]{1,0:T(8,128)(2,1)S(1)} collective-permute-done((bf16[256,512]{1,0:T(8,128)(2,1)S(1)}, bf16[256,512]{1,0:T(8,128)(2,1)S(1)}, u32[]{:S(2)}, u32[]{:S(2)}) %collective-permute-start.2) | collective-permute-done | bytes 262176 | tf_op jit(solution)/shard_map/ppermute | solution.py:229
  85.4 5.6 %collective-permute-start.4 = (bf16[256,512]{1,0:T(8,128)(2,1)S(1)}, bf16[256,512]{1,0:T(8,128)(2,1)S(1)}, u32[]{:S(2)}, u32[]{:S(2)}) collective-permute-start(bf16[256,512]{1,0:T(8,128)(2,1)S(1)} %collective-permute-done.2.refs_3_), channel_id=1, source_target_pairs={{0,1},{1,2},{2,3},{3,4},{4,5},{5,6},{6,7},{7,0},{8,9},{9,10},{10,1... | collective-permute-start | bytes 786440 | tf_op jit(solution)/shard_map/ppermute | solution.py:229
  91.0 0.0 collective-permute-done.3.refs_4_
  91.0 1.9 %collective-permute-start.5 = (bf16[256,512]{1,0:T(8,128)(2,1)S(1)}, bf16[256,512]{1,0:T(8,128)(2,1)S(1)}, u32[]{:S(2)}, u32[]{:S(2)}) collective-permute-start(bf16[256,512]{1,0:T(8,128)(2,1)S(1)} %collective-permute-done.3.refs_4_), channel_id=1, source_target_pairs={{0,7},{1,0},{2,1},{3,2},{4,3},{5,4},{6,5},{7,6},{8,15},{9,8},{10,9... | collective-permute-start | bytes 786440 | tf_op jit(solution)/shard_map/ppermute | solution.py:230
  93.0 2.2 %collective-permute-done.4.refs_5_ = bf16[256,512]{1,0:T(8,128)(2,1)S(1)} collective-permute-done((bf16[256,512]{1,0:T(8,128)(2,1)S(1)}, bf16[256,512]{1,0:T(8,128)(2,1)S(1)}, u32[]{:S(2)}, u32[]{:S(2)}) %collective-permute-start.4) | collective-permute-done | bytes 262176 | tf_op jit(solution)/shard_map/ppermute | solution.py:229
  95.2 5.6 %collective-permute-start.6 = (bf16[128,512]{1,0:T(8,128)(2,1)S(1)}, bf16[128,512]{1,0:T(8,128)(2,1)S(1)}, u32[]{:S(2)}, u32[]{:S(2)}) collective-permute-start(bf16[128,512]{1,0:T(8,128)(2,1)S(1)} %slice.8), channel_id=1, source_target_pairs={{0,1},{1,2},{2,3},{3,4},{4,5},{5,6},{6,7},{7,0},{8,9},{9,10},{10,1... | collective-permute-start | bytes 393224 | tf_op jit(solution)/shard_map/ppermute | solution.py:233
  100.8 0.0 collective-permute-done.5.refs_6_
  100.8 1.9 %collective-permute-start.7 = (bf16[128,512]{1,0:T(8,128)(2,1)S(1)}, bf16[128,512]{1,0:T(8,128)(2,1)S(1)}, u32[]{:S(2)}, u32[]{:S(2)}) collective-permute-start(bf16[128,512]{1,0:T(8,128)(2,1)S(1)} %slice.9), channel_id=1, source_target_pairs={{0,7},{1,0},{2,1},{3,2},{4,3},{5,4},{6,5},{7,6},{8,15},{9,8},{10,9... | collective-permute-start | bytes 393224 | tf_op jit(solution)/shard_map/ppermute | solution.py:234
  102.8 0.0 copy-done.6
  102.8 0.0 all-gather.2.cloned.1.call-done.refs_7_
  102.8 3.2 %shard_map.76 = (f32[256,512]{1,0:T(8,128)S(1)}, bf16[512,512]{1,0:T(8,128)(2,1)S(1)}) custom-call(s32[8]{0:T(128)S(1)} %and_select_fusion.index_ref, bf16[256,512]{1,0:T(8,128)(2,1)S(1)} %shard_map.75.refs_0_, bf16[256,512]{1,0:T(8,128)(2,1)S(1)} %collective-permute-done.refs_1_, bf16[256,512]{1,0:T(8,128)(2,1)S(1)} %collective-permute-done.1.refs_2_, ...), custom_call_target="tpu_custom_call" | custom-call | tf_op jit(solution)/shard_map/pallas_call | solution.py:237
  106.0 0.0 collective-permute-done.6.up_ref
  106.0 2.9 %collective-permute-done.7.down_ref = bf16[128,512]{1,0:T(8,128)(2,1)S(1)} collective-permute-done((bf16[128,512]{1,0:T(8,128)(2,1)S(1)}, bf16[128,512]{1,0:T(8,128)(2,1)S(1)}, u32[]{:S(2)}, u32[]{:S(2)}) %collective-permute-start.7) | collective-permute-done | bytes 131104 | tf_op jit(solution)/shard_map/ppermute | solution.py:234
  108.9 1.0 shard_map.77
  (3 shorter events, 0.0 us)
Async XLA Ops:
  6.5 96.2 %copy-start.6 = (s32[8]{0:T(128)S(1)}, s32[8]{0:T(128)}, u32[]{:S(2)}) copy-start(s32[8]{0:T(128)} %constant.24.clone) | copy-start | bytes 100
  6.5 57.5 %copy-start.5 = (f32[512]{0:T(512)S(1)}, f32[512]{0:T(512)}, u32[]{:S(2)}) copy-start(f32[512]{0:T(512)} %param.10) | copy-start | bytes 6148
  6.5 96.3 %all-gather.2.cloned.1.call-start = ((), (), s32[]{:S(2)}) async-start(), calls=%async_computation.2 | async-start | bytes 4259840 | tf_op jit(solution)/shard_map/all_gather | solution.py:195
  7.3 1.0 copy-start
  8.2 1.0 copy-start.3
  9.3 54.7 %copy-start.1 = (bf16[256,512]{1,0:T(8,128)(2,1)S(1)}, bf16[256,512]{1,0:T(8,128)(2,1)}, u32[]{:S(2)}) copy-start(bf16[256,512]{1,0:T(8,128)(2,1)} %signal_ref.3) | copy-start | bytes 786436
  9.3 54.7 %copy-start.4 = (bf16[256,512]{1,0:T(8,128)(2,1)S(1)}, bf16[256,512]{1,0:T(8,128)(2,1)}, u32[]{:S(2)}) copy-start(bf16[256,512]{1,0:T(8,128)(2,1)} %gating_ref.1) | copy-start | bytes 786436
  40.8 1.2 %copy-start.2 = (bf16[864,512]{1,0:T(8,128)(2,1)S(1)}, bf16[864,512]{1,0:T(8,128)(2,1)}, u32[]{:S(2)}) copy-start(bf16[864,512]{1,0:T(8,128)(2,1)} %constant.23.clone.table_ref) | copy-start | bytes 2654212
  64.2 10.6 %collective-permute-start = (bf16[256,512]{1,0:T(8,128)(2,1)S(1)}, bf16[256,512]{1,0:T(8,128)(2,1)S(1)}, u32[]{:S(2)}, u32[]{:S(2)}) collective-permute-start(bf16[256,512]{1,0:T(8,128)(2,1)S(1)} %shard_map.75.refs_0_), channel_id=1, source_target_pairs={{0,1},{1,2},{2,3},{3,4},{4,5},{5,6},{6,7},{7,0},{8,9},{9,10},{10,1... | collective-permute-start | bytes 786440 | tf_op jit(solution)/shard_map/ppermute | solution.py:229
  68.9 11.4 %collective-permute-start.1 = (bf16[256,512]{1,0:T(8,128)(2,1)S(1)}, bf16[256,512]{1,0:T(8,128)(2,1)S(1)}, u32[]{:S(2)}, u32[]{:S(2)}) collective-permute-start(bf16[256,512]{1,0:T(8,128)(2,1)S(1)} %shard_map.75.refs_0_), channel_id=1, source_target_pairs={{0,7},{1,0},{2,1},{3,2},{4,3},{5,4},{6,5},{7,6},{8,15},{9,8},{10,9... | collective-permute-start | bytes 786440 | tf_op jit(solution)/shard_map/ppermute | solution.py:230
  74.7 10.7 %collective-permute-start.2 = (bf16[256,512]{1,0:T(8,128)(2,1)S(1)}, bf16[256,512]{1,0:T(8,128)(2,1)S(1)}, u32[]{:S(2)}, u32[]{:S(2)}) collective-permute-start(bf16[256,512]{1,0:T(8,128)(2,1)S(1)} %collective-permute-done.refs_1_), channel_id=1, source_target_pairs={{0,1},{1,2},{2,3},{3,4},{4,5},{5,6},{6,7},{7,0},{8,9},{9,10},{10,1... | collective-permute-start | bytes 786440 | tf_op jit(solution)/shard_map/ppermute | solution.py:229
  80.3 10.7 %collective-permute-start.3 = (bf16[256,512]{1,0:T(8,128)(2,1)S(1)}, bf16[256,512]{1,0:T(8,128)(2,1)S(1)}, u32[]{:S(2)}, u32[]{:S(2)}) collective-permute-start(bf16[256,512]{1,0:T(8,128)(2,1)S(1)} %collective-permute-done.1.refs_2_), channel_id=1, source_target_pairs={{0,7},{1,0},{2,1},{3,2},{4,3},{5,4},{6,5},{7,6},{8,15},{9,8},{10,9... | collective-permute-start | bytes 786440 | tf_op jit(solution)/shard_map/ppermute | solution.py:230
  85.4 9.8 %collective-permute-start.4 = (bf16[256,512]{1,0:T(8,128)(2,1)S(1)}, bf16[256,512]{1,0:T(8,128)(2,1)S(1)}, u32[]{:S(2)}, u32[]{:S(2)}) collective-permute-start(bf16[256,512]{1,0:T(8,128)(2,1)S(1)} %collective-permute-done.2.refs_3_), channel_id=1, source_target_pairs={{0,1},{1,2},{2,3},{3,4},{4,5},{5,6},{6,7},{7,0},{8,9},{9,10},{10,1... | collective-permute-start | bytes 786440 | tf_op jit(solution)/shard_map/ppermute | solution.py:229
  91.0 9.8 %collective-permute-start.5 = (bf16[256,512]{1,0:T(8,128)(2,1)S(1)}, bf16[256,512]{1,0:T(8,128)(2,1)S(1)}, u32[]{:S(2)}, u32[]{:S(2)}) collective-permute-start(bf16[256,512]{1,0:T(8,128)(2,1)S(1)} %collective-permute-done.3.refs_4_), channel_id=1, source_target_pairs={{0,7},{1,0},{2,1},{3,2},{4,3},{5,4},{6,5},{7,6},{8,15},{9,8},{10,9... | collective-permute-start | bytes 786440 | tf_op jit(solution)/shard_map/ppermute | solution.py:230
  95.2 10.8 %collective-permute-start.6 = (bf16[128,512]{1,0:T(8,128)(2,1)S(1)}, bf16[128,512]{1,0:T(8,128)(2,1)S(1)}, u32[]{:S(2)}, u32[]{:S(2)}) collective-permute-start(bf16[128,512]{1,0:T(8,128)(2,1)S(1)} %slice.8), channel_id=1, source_target_pairs={{0,1},{1,2},{2,3},{3,4},{4,5},{5,6},{6,7},{7,0},{8,9},{9,10},{10,1... | collective-permute-start | bytes 393224 | tf_op jit(solution)/shard_map/ppermute | solution.py:233
  100.8 8.1 %collective-permute-start.7 = (bf16[128,512]{1,0:T(8,128)(2,1)S(1)}, bf16[128,512]{1,0:T(8,128)(2,1)S(1)}, u32[]{:S(2)}, u32[]{:S(2)}) collective-permute-start(bf16[128,512]{1,0:T(8,128)(2,1)S(1)} %slice.9), channel_id=1, source_target_pairs={{0,7},{1,0},{2,1},{3,2},{4,3},{5,4},{6,5},{7,6},{8,15},{9,8},{10,9... | collective-permute-start | bytes 393224 | tf_op jit(solution)/shard_map/ppermute | solution.py:234
Sparse Core Ops, SparseCore 0:
  10.7 90.0 all-gather.1
